TPU v7x, 32 devices: a whole 2x2x4 slice. The times are simulated.
32 devices in a mesh: groups: 2 (over y), streams: 8 (over z, x), segment: 2 (over core).
Axes of the slice: x: 2, y: 2, z: 4, core: 2. Of those that a mesh axis runs over, the one named last changes fastest.
Arguments:
- latent: bfloat16 [4096, 1024], P(('groups', 'streams'), 'segment'), parts along dimension 0, may hold values from -6 to 6
- conv_weight: bfloat16 [1024, 16, 512], P('streams', None, 'segment'), may hold values from -0.1875 to 0.1875
- conv_bias: float32 [512], P('segment'), may hold values from -3 to 3
- tail_cache: bfloat16 [128, 8, 512], P(('groups', 'streams'), None, 'segment'), parts along dimension 0, may hold values from -6 to 6
- input_cache: bfloat16 [128, 2, 512], P(('groups', 'streams'), None, 'segment'), parts along dimension 0, may hold values from -0.8984375 to 2
- resume_slot: int32 [128], P(('groups', 'streams')), parts along dimension 0, may hold values from -1 to 255, as said below
- res_weight: bfloat16 [3, 512, 256], P(None, 'segment'), may hold values from -0.15625 to 0.15625
- res_bias: float32 [256], replicated, may hold values from -3 to 3
- skip_weight: bfloat16 [256, 512], P(None, 'segment'), may hold values from -0.375 to 0.375
- skip_bias: float32 [512], P('segment'), may hold values from -3 to 3
Outputs:
- decoded: bfloat16 [4096, 8, 512], P(('groups', 'streams'), None, 'segment'), parts along dimension 0
- new_tail: bfloat16 [4096, 8, 512], P(('groups', 'streams'), None, 'segment'), parts along dimension 0
There are 2 independent parts, one for each index of `groups`. A program takes and returns all parts, laid end to end along the dimension named above; an argument that names none is the same for every part. Nothing has to cross between parts.
Inputs may be any that keep to these rules, and one draw needn't show every extreme that they name: `resume_slot`: slot k of an owner device's store serves decoder device k // 1 of the same index range; an entry is -1 (slot unused) or the position, among that decoder device's 256 rows in decoder order, of the session that resumes from it. No decoder row is named by two slots. In every draw there is one decoder device all of whose reserved slots are in use (none is -1).
All inputs are finite; a program needn't handle non-finite values.
Results may differ from a plain program's by a relative error of at most 0.0042.
Values may be sent and summed in bfloat16 or wider, within the bound.
No kernel may reach another device: no remote copies, remote signals or barrier semaphores. Data moves between devices by JAX's collectives and lax.ppermute only.
A program may use at most 64 MiB of HBM per device.

v0:
```python
import functools

import jax
import jax.numpy as jnp
from jax import lax
from jax.experimental import pallas as pl
from jax.experimental.pallas import tpu as pltpu
from jax.sharding import PartitionSpec as P

VMEM_LIMIT = 16 * 1024 * 1024
F32 = jnp.float32
BF16 = jnp.bfloat16
VMEM = pl.BlockSpec(memory_space=pltpu.VMEM)


def apply_elu(values):
    return jnp.where(values > 0, values, jnp.exp(jnp.minimum(values, 0.0)) - 1.0)


def ring_order(count):
    return [2 * p if p < count // 2 else 2 * (count - 1 - p) + 1 for p in range(count)]


def ring_place(stream, count):
    return jnp.where(stream % 2 == 0, stream // 2, count - 1 - stream // 2)


def ring_stream(place, count):
    return jnp.where(place < count // 2, 2 * place, 2 * (count - 1 - place) + 1)


def spread_kernel(count, steps, *refs):
    blocks = refs[: len(steps)]
    sides, (home_ref, *away_refs) = refs[len(steps) : len(steps) + 4], refs[len(steps) + 4 : -3]
    kernel_rows, inputs, sems = refs[-3:]
    taps = kernel_rows.shape[0]
    rows = blocks[0].shape[-2]
    core = lax.axis_index("segment")
    place = ring_place(lax.axis_index("streams"), count)
    copies = []
    for slot, (step, block) in enumerate(zip(steps, blocks)):
        if step is None:
            source, target = block, kernel_rows
        else:
            distance, passed = step
            taker = 1 - core if passed else core
            stream = ring_stream(
                lax.rem(place + (2 * taker - 1) * distance + count, count), count
            )
            source = block if len(block.shape) == 3 else block.at[passed]
            part = source.shape[0]
            first = 0 if part == taps else taker * part
            target = kernel_rows.at[
                pl.ds(first, part), pl.ds(pl.multiple_of(stream * rows, rows), rows), :
            ]
        copy = pltpu.make_async_copy(source, target, sems.at[slot])
        copy.start()
        copies.append(copy)
    sessions, half = sides[0].shape
    for index, side in enumerate(sides):
        column = core if index % 2 == 0 else 1 - core
        first = index // 2 * sessions
        inputs[first : first + sessions, pl.ds(pl.multiple_of(column * half, half), half)] = side[...]
    for copy in copies:
        copy.wait()

    for part, away_ref in enumerate(away_refs):

        @pl.loop(0, away_ref.shape[0])
        def _(index):
            tap = part * away_ref.shape[0] + index
            product = jnp.dot(inputs[...], kernel_rows[tap], preferred_element_type=F32)
            home_ref[tap] = product[:sessions].astype(home_ref.dtype)
            away_ref[index] = product[sessions:].astype(away_ref.dtype)


def spread_taps(sides, blocks, steps, count, home_type):
    taps, _, width = blocks[0].shape
    sessions, depth = sides[0].shape[0], 2 * sides[0].shape[1]
    return pl.pallas_call(
        functools.partial(spread_kernel, count, steps),
        out_shape=(
            jax.ShapeDtypeStruct((taps, sessions, width), home_type),
            jax.ShapeDtypeStruct((taps // 2, sessions, width), BF16),
            jax.ShapeDtypeStruct((taps // 2, sessions, width), BF16),
        ),
        in_specs=[pl.BlockSpec(memory_space=pl.ANY)] * len(blocks) + [VMEM] * 4,
        out_specs=(VMEM, VMEM, VMEM),
        scratch_shapes=[
            pltpu.VMEM((taps, depth, width), BF16),
            pltpu.VMEM((2 * sessions, depth), BF16),
            pltpu.SemaphoreType.DMA((len(blocks),)),
        ],
        compiler_params=pltpu.CompilerParams(vmem_limit_bytes=VMEM_LIMIT),
        cost_estimate=pl.CostEstimate(
            flops=4 * taps * sessions * depth * width,
            bytes_accessed=2 * taps * depth * width + 4 * sessions * depth + 6 * taps * sessions * width,
            transcendentals=0,
        ),
    )(*blocks, *sides)


def each_step(group, own_ref, other_refs):
    taps = own_ref.shape[0]
    for tap in range(taps):
        yield group * taps + tap, own_ref[tap].astype(F32)
    for tap in range(taps):
        part, index = divmod(tap, other_refs[0].shape[0])
        yield (1 - group) * taps + tap, other_refs[part][index].astype(F32)


def excite_kernel(group_ref, own_ref, first_ref, second_ref, prev_ref, bias_ref, window_ref):
    steps = 2 * own_ref.shape[0]
    history = prev_ref.shape[0] - steps
    for step in range(history):
        window_ref[step] = prev_ref[steps + step]
    for step, value in each_step(group_ref[0], own_ref, (first_ref, second_ref)):
        up = value + prev_ref[step].astype(F32) + bias_ref[...]
        window_ref[history + step] = apply_elu(up).astype(BF16)


def excite(group, own, other, prev, bias):
    return pl.pallas_call(
        excite_kernel,
        out_shape=jax.ShapeDtypeStruct(prev.shape, BF16),
        in_specs=[pl.BlockSpec(memory_space=pltpu.SMEM)] + [VMEM] * 5,
        out_specs=VMEM,
        compiler_params=pltpu.CompilerParams(vmem_limit_bytes=VMEM_LIMIT),
    )(group, own, *other, prev, bias)


def residual_kernel(
    group_ref,
    own_ref,
    first_ref,
    second_ref,
    prev_ref,
    mine_ref,
    theirs_ref,
    bias_ref,
    res_mine_ref,
    res_theirs_ref,
    res_bias_ref,
    skip_ref,
    skip_bias_ref,
    out_ref,
    products,
    frames,
):
    taps, block, width = own_ref.shape
    steps = 2 * taps
    branch = None
    for source, weights in ((mine_ref, res_mine_ref), (theirs_ref, res_theirs_ref)):
        for offset in range(weights.shape[0]):
            term = jnp.dot(
                source[offset : offset + steps].reshape(steps * block, width),
                weights[offset],
                preferred_element_type=F32,
            )
            branch = term if branch is None else branch + term
    hidden = apply_elu(branch + res_bias_ref[...]).astype(BF16)
    projected = jnp.dot(hidden, skip_ref[...], preferred_element_type=F32)
    products[...] = projected.reshape(products.shape)
    for step, value in each_step(group_ref[0], own_ref, (first_ref, second_ref)):
        up = value + prev_ref[step].astype(F32) + bias_ref[...]
        mixed = up + products[step] + skip_bias_ref[...]
        for part in range(width // 128):
            frames.at[part][pl.ds(step, block, stride=steps), :] = mixed[
                :, part * 128 : (part + 1) * 128
            ]
    for part in range(width // 128):
        out_ref[:, part * 128 : (part + 1) * 128] = frames[part].astype(BF16)


def residual(group, own, other, prev, mine, theirs, *parameters):
    taps, sessions, width = own.shape
    steps, block = 2 * taps, sessions // 4

    def blocks(array):
        return pl.BlockSpec((array.shape[0], block, width), lambda i: (0, i, 0))

    arrays = (own, *other, prev, mine, theirs)
    return pl.pallas_call(
        residual_kernel,
        out_shape=jax.ShapeDtypeStruct((sessions * steps, width), BF16),
        grid=(4,),
        in_specs=[pl.BlockSpec(memory_space=pltpu.SMEM)]
        + [blocks(array) for array in arrays]
        + [VMEM] * len(parameters),
        out_specs=pl.BlockSpec((block * steps, width), lambda i: (i, 0)),
        scratch_shapes=[
            pltpu.VMEM((steps, block, width), F32),
            pltpu.VMEM((width // 128, block * steps, 128), F32),
        ],
        compiler_params=pltpu.CompilerParams(vmem_limit_bytes=VMEM_LIMIT),
    )(group, *arrays, *parameters)


def weave_kernel(group_ref, own_ref, first_ref, second_ref, out_ref, frames):
    taps, block, width = own_ref.shape
    for step, value in each_step(group_ref[0], own_ref, (first_ref, second_ref)):
        for part in range(width // 128):
            frames.at[part][pl.ds(step, block, stride=2 * taps), :] = value[
                :, part * 128 : (part + 1) * 128
            ]
    for part in range(width // 128):
        out_ref[:, part * 128 : (part + 1) * 128] = frames[part].astype(BF16)


def weave(group, own, other):
    taps, sessions, width = own.shape
    steps, block = 2 * taps, sessions // 4
    arrays = (own, *other)
    taken = [pl.BlockSpec((array.shape[0], block, width), lambda i: (0, i, 0)) for array in arrays]
    return pl.pallas_call(
        weave_kernel,
        out_shape=jax.ShapeDtypeStruct((sessions * steps, width), BF16),
        grid=(4,),
        in_specs=[pl.BlockSpec(memory_space=pltpu.SMEM)] + taken,
        out_specs=pl.BlockSpec((block * steps, width), lambda i: (i, 0)),
        scratch_shapes=[pltpu.VMEM((width // 128, block * steps, 128), F32)],
        compiler_params=pltpu.CompilerParams(vmem_limit_bytes=VMEM_LIMIT),
    )(group, *arrays)


def swap(value, axis):
    return lax.ppermute(value, axis, [(0, 1), (1, 0)])


def after(value, earlier):
    return lax.optimization_barrier((value, earlier))[0]


class Ring:
    def __init__(self, count, own, other):
        order = ring_order(count)
        self.count = count
        self.pairs = []
        for p in range(count):
            here, there = order[p], order[(p + 1) % count]
            self.pairs += [(2 * here, 2 * there), (2 * there + 1, 2 * here + 1)]
        self.item = jnp.stack([own, other])
        self.blocks, self.steps, self.rounds = [own], [(0, 0)], 0

    def round(self, earlier=None, passed_after=None):
        self.rounds += 1
        item = self.item
        if 2 * self.rounds == self.count:
            part = item.shape[1] // 2
            item = lax.dynamic_slice_in_dim(item, lax.axis_index("segment") * part, part, axis=1)
        if earlier is not None:
            item = after(item, earlier)
        item = lax.ppermute(item, ("streams", "segment"), self.pairs)
        self.item = item
        given = item if passed_after is None else after(item, passed_after)
        self.blocks += [item, swap(given, "segment")]
        self.steps += [(self.rounds, 0), (self.rounds, 1)]
        return item


def local(
    count,
    latent,
    conv_weight,
    conv_bias,
    tail_cache,
    input_cache,
    resume_slot,
    res_weight,
    res_bias,
    skip_weight,
    skip_bias,
):
    group = lax.axis_index("groups")
    group_word = group[None].astype(jnp.int32)
    rows, tap_count, width = conv_weight.shape
    sessions = latent.shape[0]
    taps = tap_count // 4

    halves = []
    for first in (0, tap_count // 2):
        part = lax.dynamic_slice_in_dim(conv_weight, first + group * taps, taps, axis=1)
        halves.append(part.transpose(1, 0, 2))

    use_ring = rows % 128 == 0 and count % 2 == 0 and count > 4
    if use_ring:
        other = swap(halves[0], "segment")
        prepared = swap(after(halves[1], other), "segment")
        up_ring, tail_ring = Ring(count, halves[0], other), Ring(count, halves[1], prepared)
    else:
        prepared = halves[1]

    portion = sessions // count
    cap = tail_cache.shape[0] // count
    half_taps, history = tail_cache.shape[1], input_cache.shape[1]
    slot_step = jnp.broadcast_to(
        resume_slot.astype(BF16)[:, None, None], (count * cap, 1, width)
    )
    filler = jnp.zeros((count * cap, half_taps - history - 1, width), BF16)
    beside = jnp.concatenate([input_cache, slot_step, filler], axis=1)
    stored = jnp.concatenate([tail_cache, beside], axis=2).reshape(count, cap * half_taps, 2 * width)
    parcel = jnp.concatenate([latent.reshape(count, portion, 2 * width), stored], axis=1)
    parcel = after(parcel, prepared)
    parcel = lax.all_to_all(parcel, "streams", split_axis=0, concat_axis=0, tiled=True)
    handed = parcel[:, :portion].reshape(sessions, 2 * width)
    stored = parcel[:, portion:].reshape(count * cap, half_taps, 2 * width)

    near_half = apply_elu(handed.astype(F32)).astype(BF16)
    far_half = swap(near_half, "groups")
    sides = (near_half, swap(near_half, "segment"), far_half, swap(far_half, "segment"))

    slots = stored[:, history, width:].astype(jnp.int32)[:, :1]
    one_hot = (slots == jnp.arange(sessions, dtype=jnp.int32)[None, :]).astype(BF16)
    packed = jnp.concatenate([stored[:, :, :width], stored[:, :history, width:]], axis=1)
    prev = jnp.einsum("js,jkc->ksc", one_hot, packed, preferred_element_type=F32).astype(BF16)

    res_theirs = swap(res_weight, "segment")

    if use_ring:
        last = count // 2 - 1
        leading = [up_ring.round(far_half if r == last else None) for r in range(last + 1)]
        for r in range(last - 1):
            item = tail_ring.round(leading[min(r + 1, last)])
            if r == 0:
                up_ring.blocks[0] = after(up_ring.blocks[0], item)
        own_up, *away_up = spread_taps(sides, up_ring.blocks, up_ring.steps, count, F32)
        tail_ring.round(away_up)
        other_up = [swap(part, "groups") for part in away_up]
        tail_ring.round(other_up[0], passed_after=other_up[1])
        own_tail, *away_tail = spread_taps(sides, tail_ring.blocks, tail_ring.steps, count, BF16)
    else:
        whole = [lax.all_gather(own, "streams", axis=1, tiled=True) for own in halves]
        own_up, *away_up = spread_taps(sides, whole[:1], [None], count, F32)
        other_up = [swap(part, "groups") for part in away_up]
        own_tail, *away_tail = spread_taps(sides, whole[1:], [None], count, BF16)
    other_tail = [swap(part, "groups") for part in away_tail]

    own_up = after(own_up, (away_tail, res_theirs))
    bias = conv_bias[None]
    mine = excite(group_word, own_up, other_up, prev, bias)
    theirs = swap(mine, "segment")
    decoded = residual(
        group_word,
        own_up,
        other_up,
        prev,
        mine,
        theirs,
        bias,
        res_weight,
        res_theirs,
        res_bias[None],
        skip_weight,
        skip_bias[None],
    )
    decoded, other_tail = lax.optimization_barrier((decoded, other_tail))
    new_tail = weave(group_word, own_tail, other_tail)
    shape = (sessions, half_taps, width)
    return decoded.reshape(shape), new_tail.reshape(shape)


def solution(mesh):
    placed = (
        P(("groups", "streams"), "segment"),
        P("streams", None, "segment"),
        P("segment"),
        P(("groups", "streams"), None, "segment"),
        P(("groups", "streams"), None, "segment"),
        P(("groups", "streams")),
        P(None, "segment", None),
        P(),
        P(None, "segment"),
        P("segment"),
    )
    return jax.shard_map(
        functools.partial(local, mesh.shape["streams"]),
        mesh=mesh,
        in_specs=placed,
        out_specs=(
            P(("groups", "streams"), None, "segment"),
            P(("groups", "streams"), None, "segment"),
        ),
        check_vma=False,
    )
```

profile of v0, /device:TPU:0, one launch (start us, length us, event | category | flops | bytes accessed | tf_op | source)
XLA Modules:
  0.0 89.5 jit_solution(2185249676605479859)
XLA Ops:
  0.6 1.5 %constant_dynamic-slice_fusion.2 = (bf16[128,4,256]{2,1,0:T(4,128)(2,1)S(1)}, bf16[128,4,256]{2,1,0:T(4,128)(2,1)S(1)}) fusion(bf16[128,16,256]{2,1,0:T(8,128)(2,1)} %param.11, s32[]{:T(128)S(6)} %select_n.15, s32[]{:T(128)S(6)} %select_n.14), kind=kLoop, calls=%fused_computation.24 | loop fusion | bytes 1048584 | tf_op jit(solution)/shard_map/dynamic_slice | solution.py:282
  2.1 0.0 copy-start.8
  2.2 0.0 copy-start.7
  2.2 0.5 collective-permute-start
  2.7 1.2 %collective-permute-done = bf16[4,128,256]{2,1,0:T(8,128)(2,1)S(1)} collective-permute-done((bf16[4,128,256]{2,1,0:T(8,128)(2,1)S(1)}, bf16[4,128,256]{2,1,0:T(8,128)(2,1)S(1)}, u32[]{:S(2)}, u32[]{:S(2)}) %collective-permute-start) | collective-permute-done | bytes 262176 | tf_op jit(solution)/shard_map/ppermute | solution.py:227
  3.9 0.1 pad_maximum_fusion.1
  3.9 3.0 %collective-permute-start.2 = (bf16[2,4,128,256]{3,2,1,0:T(8,128)(2,1)S(1)}, bf16[2,4,128,256]{3,2,1,0:T(8,128)(2,1)S(1)}, u32[]{:S(2)}, u32[]{:S(2)}) collective-permute-start(bf16[2,4,128,256]{3,2,1,0:T(8,128)(2,1)S(1)} %pad_maximum_fusion.1), channel_id=1, source_target_pairs={{0,4},{5,1},{4,8},{9,5},{8,12},{13,9},{12,14},{15,13},{14,10},{11,... | collective-permute-start | bytes 1572872 | tf_op jit(solution)/shard_map/ppermute | solution.py:253
  7.0 0.1 collective-permute-start.1
  7.1 6.9 %collective-permute-done.2.refs_1_ = bf16[2,4,128,256]{3,2,1,0:T(8,128)(2,1)S(1)} collective-permute-done((bf16[2,4,128,256]{3,2,1,0:T(8,128)(2,1)S(1)}, bf16[2,4,128,256]{3,2,1,0:T(8,128)(2,1)S(1)}, u32[]{:S(2)}, u32[]{:S(2)}) %collective-permute-start.2) | collective-permute-done | bytes 524320 | tf_op jit(solution)/shard_map/ppermute | solution.py:253
  14.0 2.1 %collective-permute-start.3 = (bf16[2,4,128,256]{3,2,1,0:T(8,128)(2,1)S(1)}, bf16[2,4,128,256]{3,2,1,0:T(8,128)(2,1)S(1)}, u32[]{:S(2)}, u32[]{:S(2)}) collective-permute-start(bf16[2,4,128,256]{3,2,1,0:T(8,128)(2,1)S(1)} %collective-permute-done.2.refs_1_), channel_id=1, source_target_pairs={{0,4},{5,1},{4,8},{9,5},{8,12},{13,9},{12,14},{15,13},{14,10},{11,... | collective-permute-start | bytes 1572872 | tf_op jit(solution)/shard_map/ppermute | solution.py:253
  16.1 0.1 broadcast_in_dim.23
  16.2 0.8 maximum_maximum_fusion
  17.0 4.8 %all-to-all-start = ((bf16[8,40,512]{2,1,0:T(8,128)(2,1)}), bf16[8,40,512]{2,1,0:T(8,128)(2,1)S(1)}, u32[]{:S(2)}, u32[]{:S(2)}) async-start(bf16[8,40,512]{2,1,0:T(8,128)(2,1)} %maximum_maximum_fusion), calls=%async_computation | async-start | bytes 655360 | tf_op jit(solution)/shard_map/all_to_all | solution.py:304
  21.8 2.6 %collective-permute-done.3.refs_3_ = bf16[2,4,128,256]{3,2,1,0:T(8,128)(2,1)S(1)} collective-permute-done((bf16[2,4,128,256]{3,2,1,0:T(8,128)(2,1)S(1)}, bf16[2,4,128,256]{3,2,1,0:T(8,128)(2,1)S(1)}, u32[]{:S(2)}, u32[]{:S(2)}) %collective-permute-start.3) | collective-permute-done | bytes 524320 | tf_op jit(solution)/shard_map/ppermute | solution.py:253
  24.4 3.4 %collective-permute-start.7 = (bf16[2,4,128,256]{3,2,1,0:T(8,128)(2,1)S(1)}, bf16[2,4,128,256]{3,2,1,0:T(8,128)(2,1)S(1)}, u32[]{:S(2)}, u32[]{:S(2)}) collective-permute-start(bf16[2,4,128,256]{3,2,1,0:T(8,128)(2,1)S(1)} %collective-permute-done.3.refs_3_), channel_id=1, source_target_pairs={{0,4},{5,1},{4,8},{9,5},{8,12},{13,9},{12,14},{15,13},{14,10},{11,... | collective-permute-start | bytes 1572872 | tf_op jit(solution)/shard_map/ppermute | solution.py:253
  27.9 0.8 pad_maximum_fusion
  28.7 3.2 %collective-permute-start.4 = (bf16[2,4,128,256]{3,2,1,0:T(8,128)(2,1)}, bf16[2,4,128,256]{3,2,1,0:T(8,128)(2,1)S(1)}, u32[]{:S(2)}, u32[]{:S(2)}) collective-permute-start(bf16[2,4,128,256]{3,2,1,0:T(8,128)(2,1)} %pad_maximum_fusion), channel_id=1, source_target_pairs={{0,4},{5,1},{4,8},{9,5},{8,12},{13,9},{12,14},{15,13},{14,10},{11,... | collective-permute-start | bytes 1572872 | tf_op jit(solution)/shard_map/ppermute | solution.py:253
  31.9 1.2 %all-to-all-done = bf16[8,40,512]{2,1,0:T(8,128)(2,1)S(1)} async-done(((bf16[8,40,512]{2,1,0:T(8,128)(2,1)}), bf16[8,40,512]{2,1,0:T(8,128)(2,1)S(1)}, u32[]{:S(2)}, u32[]{:S(2)}) %all-to-all-start) | async-done | bytes 327712 | tf_op jit(solution)/shard_map/all_to_all | solution.py:304
  33.1 0.1 fusion.3.refs_9_
  33.3 1.6 %collective-permute-start.9 = (bf16[256,512]{1,0:T(8,128)(2,1)S(1)}, bf16[256,512]{1,0:T(8,128)(2,1)S(1)}, u32[]{:S(2)}, u32[]{:S(2)}) collective-permute-start(bf16[256,512]{1,0:T(8,128)(2,1)S(1)} %fusion.3.refs_9_), channel_id=1, source_target_pairs={{0,16},{16,0},{1,17},{17,1},{2,18},{18,2},{3,19},{19,3},{4,20},{20... | collective-permute-start | bytes 786440 | tf_op jit(solution)/shard_map/ppermute | solution.py:227
  34.9 0.5 collective-permute-start.6
  35.4 5.5 %collective-permute-done.9.refs_11_ = bf16[256,512]{1,0:T(8,128)(2,1)S(1)} collective-permute-done((bf16[256,512]{1,0:T(8,128)(2,1)S(1)}, bf16[256,512]{1,0:T(8,128)(2,1)S(1)}, u32[]{:S(2)}, u32[]{:S(2)}) %collective-permute-start.9) | collective-permute-done | bytes 262176 | tf_op jit(solution)/shard_map/ppermute | solution.py:227
  40.9 2.6 %collective-permute-start.15 = (bf16[2,4,128,256]{3,2,1,0:T(8,128)(2,1)S(1)}, bf16[2,4,128,256]{3,2,1,0:T(8,128)(2,1)S(1)}, u32[]{:S(2)}, u32[]{:S(2)}) collective-permute-start(bf16[2,4,128,256]{3,2,1,0:T(8,128)(2,1)S(1)} %collective-permute-done.4.refs_1_), channel_id=1, source_target_pairs={{0,4},{5,1},{4,8},{9,5},{8,12},{13,9},{12,14},{15,13},{14,10},{11,... | collective-permute-start | bytes 1572872 | tf_op jit(solution)/shard_map/ppermute | solution.py:253
  43.5 3.7 %collective-permute-done.10.refs_7_ = bf16[2,2,128,256]{3,2,1,0:T(8,128)(2,1)S(1)} collective-permute-done((bf16[2,2,128,256]{3,2,1,0:T(8,128)(2,1)S(1)}, bf16[2,2,128,256]{3,2,1,0:T(8,128)(2,1)S(1)}, u32[]{:S(2)}, u32[]{:S(2)}) %collective-permute-start.10) | collective-permute-done | bytes 262176 | tf_op jit(solution)/shard_map/ppermute | solution.py:253
  47.3 1.5 %collective-permute-done.11.refs_8_ = bf16[2,2,128,256]{3,2,1,0:T(8,128)(2,1)S(1)} collective-permute-done((bf16[2,2,128,256]{3,2,1,0:T(8,128)(2,1)S(1)}, bf16[2,2,128,256]{3,2,1,0:T(8,128)(2,1)S(1)}, u32[]{:S(2)}, u32[]{:S(2)}) %collective-permute-start.11) | collective-permute-done | bytes 262176 | tf_op jit(solution)/shard_map/ppermute | solution.py:227
  48.8 2.8 %shard_map.113 = (f32[4,256,256]{2,1,0:T(8,128)S(1)}, bf16[2,256,256]{2,1,0:T(8,128)(2,1)S(1)}, bf16[2,256,256]{2,1,0:T(8,128)(2,1)S(1)}) custom-call(bf16[4,128,256]{2,1,0:T(8,128)(2,1)S(1)} %bitcast.37, bf16[2,4,128,256]{3,2,1,0:T(8,128)(2,1)S(1)} %collective-permute-done.2.refs_1_, bf16[2,4,128,256]{3,2,1,0:T(8,128)(2,1)} %collective-permute-done.5.refs_2_, ...), custom_call_target="tpu_custom_call" | custom-call | flops 1073741824 | bytes 4718592 | tf_op jit(solution)/shard_map/pallas_call | solution.py:80
  51.6 1.2 %collective-permute-done.15.refs_3_ = bf16[2,4,128,256]{3,2,1,0:T(8,128)(2,1)S(1)} collective-permute-done((bf16[2,4,128,256]{3,2,1,0:T(8,128)(2,1)S(1)}, bf16[2,4,128,256]{3,2,1,0:T(8,128)(2,1)S(1)}, u32[]{:S(2)}, u32[]{:S(2)}) %collective-permute-start.15) | collective-permute-done | bytes 524320 | tf_op jit(solution)/shard_map/ppermute | solution.py:253
  52.9 1.5 %collective-permute-start.19 = (bf16[2,256,256]{2,1,0:T(8,128)(2,1)S(1)}, bf16[2,256,256]{2,1,0:T(8,128)(2,1)S(1)}, u32[]{:S(2)}, u32[]{:S(2)}) collective-permute-start(bf16[2,256,256]{2,1,0:T(8,128)(2,1)S(1)} %get-tuple-element.28), channel_id=1, source_target_pairs={{0,16},{16,0},{1,17},{17,1},{2,18},{18,2},{3,19},{19,3},{4,20},{20... | collective-permute-start | bytes 786440 | tf_op jit(solution)/shard_map/ppermute | solution.py:227
  54.4 0.5 collective-permute-start.21
  54.9 7.2 %collective-permute-done.17.refs_5_ = bf16[2,4,128,256]{3,2,1,0:T(8,128)(2,1)S(1)} collective-permute-done((bf16[2,4,128,256]{3,2,1,0:T(8,128)(2,1)S(1)}, bf16[2,4,128,256]{3,2,1,0:T(8,128)(2,1)S(1)}, u32[]{:S(2)}, u32[]{:S(2)}) %collective-permute-start.17) | collective-permute-done | bytes 524320 | tf_op jit(solution)/shard_map/ppermute | solution.py:253
  62.1 0.0 collective-permute-done.19.first_ref
  62.1 2.2 %collective-permute-start.20 = (bf16[2,2,128,256]{3,2,1,0:T(8,128)(2,1)S(1)}, bf16[2,2,128,256]{3,2,1,0:T(8,128)(2,1)S(1)}, u32[]{:S(2)}, u32[]{:S(2)}) collective-permute-start(bf16[2,2,128,256]{3,2,1,0:T(8,128)(2,1)S(1)} %constant_dynamic-slice_fusion), channel_id=1, source_target_pairs={{0,4},{5,1},{4,8},{9,5},{8,12},{13,9},{12,14},{15,13},{14,10},{11,... | collective-permute-start | bytes 786440 | tf_op jit(solution)/shard_map/ppermute | solution.py:253
  64.3 0.5 collective-permute-start.16
  64.8 0.9 %collective-permute-done.21.second_ref = bf16[2,256,256]{2,1,0:T(8,128)(2,1)S(1)} collective-permute-done((bf16[2,256,256]{2,1,0:T(8,128)(2,1)S(1)}, bf16[2,256,256]{2,1,0:T(8,128)(2,1)S(1)}, u32[]{:S(2)}, u32[]{:S(2)}) %collective-permute-start.21) | collective-permute-done | bytes 262176 | tf_op jit(solution)/shard_map/ppermute | solution.py:227
  65.8 2.7 %collective-permute-done.20.refs_7_ = bf16[2,2,128,256]{3,2,1,0:T(8,128)(2,1)S(1)} collective-permute-done((bf16[2,2,128,256]{3,2,1,0:T(8,128)(2,1)S(1)}, bf16[2,2,128,256]{3,2,1,0:T(8,128)(2,1)S(1)}, u32[]{:S(2)}, u32[]{:S(2)}) %collective-permute-start.20) | collective-permute-done | bytes 262176 | tf_op jit(solution)/shard_map/ppermute | solution.py:253
  68.5 0.1 convert_reduce_fusion
  68.7 0.6 fusion.prev_ref
  69.3 0.7 collective-permute-done.22.refs_8_
  70.0 2.3 %shard_map.114 = (bf16[4,256,256]{2,1,0:T(8,128)(2,1)S(1)}, bf16[2,256,256]{2,1,0:T(8,128)(2,1)S(1)}, bf16[2,256,256]{2,1,0:T(8,128)(2,1)S(1)}) custom-call(bf16[4,128,256]{2,1,0:T(8,128)(2,1)S(1)} %bitcast.34, bf16[2,4,128,256]{3,2,1,0:T(8,128)(2,1)S(1)} %collective-permute-done.4.refs_1_, bf16[2,4,128,256]{3,2,1,0:T(8,128)(2,1)S(1)} %collective-permute-done.14.refs_2_, ...), custom_call_target="tpu_custom_call" | custom-call | flops 1073741824 | bytes 4718592 | tf_op jit(solution)/shard_map/pallas_call | solution.py:80
  72.4 0.7 shard_map.115.mine_ref
  73.1 0.2 collective-permute-start.24
  73.3 1.5 %collective-permute-start.25 = (bf16[2,256,256]{2,1,0:T(8,128)(2,1)S(1)}, bf16[2,256,256]{2,1,0:T(8,128)(2,1)S(1)}, u32[]{:S(2)}, u32[]{:S(2)}) collective-permute-start(bf16[2,256,256]{2,1,0:T(8,128)(2,1)S(1)} %get-tuple-element.33), channel_id=1, source_target_pairs={{0,16},{16,0},{1,17},{17,1},{2,18},{18,2},{3,19},{19,3},{4,20},{20... | collective-permute-start | bytes 786440 | tf_op jit(solution)/shard_map/ppermute | solution.py:227
  74.8 0.5 collective-permute-start.26
  75.3 0.9 collective-permute-done.24.theirs_ref
  76.2 5.1 %shard_map.116 = bf16[2048,256]{1,0:T(8,128)(2,1)} custom-call(s32[1]{0:T(128)} %bitcast.group_ref, f32[4,256,256]{2,1,0:T(8,128)S(1)} %get-tuple-element.35.own_ref, bf16[2,256,256]{2,1,0:T(8,128)(2,1)S(1)} %collective-permute-done.19.first_ref, bf16[2,256,256]{2,1,0:T(8,128)(2,1)S(1)} %collective-permute-done.21.second_ref, ...), custom_call_target="tpu_custom_call" | custom-call | tf_op jit(solution)/shard_map/pallas_call | solution.py:183
  81.3 1.1 %collective-permute-done.25.first_ref = bf16[2,256,256]{2,1,0:T(8,128)(2,1)S(1)} collective-permute-done((bf16[2,256,256]{2,1,0:T(8,128)(2,1)S(1)}, bf16[2,256,256]{2,1,0:T(8,128)(2,1)S(1)}, u32[]{:S(2)}, u32[]{:S(2)}) %collective-permute-start.25) | collective-permute-done | bytes 262176 | tf_op jit(solution)/shard_map/ppermute | solution.py:227
  82.4 5.1 %collective-permute-done.26.second_ref = bf16[2,256,256]{2,1,0:T(8,128)(2,1)S(1)} collective-permute-done((bf16[2,256,256]{2,1,0:T(8,128)(2,1)S(1)}, bf16[2,256,256]{2,1,0:T(8,128)(2,1)S(1)}, u32[]{:S(2)}, u32[]{:S(2)}) %collective-permute-start.26) | collective-permute-done | bytes 262176 | tf_op jit(solution)/shard_map/ppermute | solution.py:227
  87.5 2.0 %shard_map.117 = bf16[2048,256]{1,0:T(8,128)(2,1)} custom-call(s32[1]{0:T(128)} %bitcast.group_ref, bf16[4,256,256]{2,1,0:T(8,128)(2,1)S(1)} %get-tuple-element.37.own_ref, bf16[2,256,256]{2,1,0:T(8,128)(2,1)S(1)} %collective-permute-done.25.first_ref, bf16[2,256,256]{2,1,0:T(8,128)(2,1)S(1)} %collective-permute-done.26.second_ref), custom_call_target="tpu_custom_call" | custom-call | tf_op jit(solution)/shard_map/pallas_call | solution.py:215
  (53 shorter events, 0.3 us)
Async XLA Ops:
  2.1 4.9 %copy-start.8 = (s32[8]{0:T(128)S(1)}, s32[8]{0:T(128)}, u32[]{:S(2)}) copy-start(s32[8]{0:T(128)} %param.15) | copy-start | bytes 100
  2.1 14.1 %copy-start.5 = (bf16[256,512]{1,0:T(8,128)(2,1)S(1)}, bf16[256,512]{1,0:T(8,128)(2,1)}, u32[]{:S(2)}) copy-start(bf16[256,512]{1,0:T(8,128)(2,1)} %param.10) | copy-start | bytes 786436
  2.1 14.1 %copy-start.6 = (bf16[8,8,256]{2,1,0:T(8,128)(2,1)S(1)}, bf16[8,8,256]{2,1,0:T(8,128)(2,1)}, u32[]{:S(2)}) copy-start(bf16[8,8,256]{2,1,0:T(8,128)(2,1)} %param.13) | copy-start | bytes 98308
  2.2 14.0 %copy-start.7 = (bf16[8,2,256]{2,1,0:T(2,128)(2,1)S(1)}, bf16[8,2,256]{2,1,0:T(2,128)(2,1)}, u32[]{:S(2)}) copy-start(bf16[8,2,256]{2,1,0:T(2,128)(2,1)} %param.14) | copy-start | bytes 24580
  2.2 1.7 %collective-permute-start = (bf16[4,128,256]{2,1,0:T(8,128)(2,1)S(1)}, bf16[4,128,256]{2,1,0:T(8,128)(2,1)S(1)}, u32[]{:S(2)}, u32[]{:S(2)}) collective-permute-start(bf16[4,128,256]{2,1,0:T(8,128)(2,1)S(1)} %bitcast.35), channel_id=1, source_target_pairs={{0,1},{1,0},{2,3},{3,2},{4,5},{5,4},{6,7},{7,6},{8,9},{9,8},{10,11... | collective-permute-start | bytes 786440 | tf_op jit(solution)/shard_map/ppermute | solution.py:227
  3.9 10.1 %collective-permute-start.2 = (bf16[2,4,128,256]{3,2,1,0:T(8,128)(2,1)S(1)}, bf16[2,4,128,256]{3,2,1,0:T(8,128)(2,1)S(1)}, u32[]{:S(2)}, u32[]{:S(2)}) collective-permute-start(bf16[2,4,128,256]{3,2,1,0:T(8,128)(2,1)S(1)} %pad_maximum_fusion.1), channel_id=1, source_target_pairs={{0,4},{5,1},{4,8},{9,5},{8,12},{13,9},{12,14},{15,13},{14,10},{11,... | collective-permute-start | bytes 1572872 | tf_op jit(solution)/shard_map/ppermute | solution.py:253
  7.0 10.1 %collective-permute-start.1 = (bf16[4,128,256]{2,1,0:T(8,128)(2,1)S(1)}, bf16[4,128,256]{2,1,0:T(8,128)(2,1)S(1)}, u32[]{:S(2)}, u32[]{:S(2)}) collective-permute-start(bf16[4,128,256]{2,1,0:T(8,128)(2,1)S(1)} %bitcast.32), channel_id=1, source_target_pairs={{0,1},{1,0},{2,3},{3,2},{4,5},{5,4},{6,7},{7,6},{8,9},{9,8},{10,11... | collective-permute-start | bytes 786440 | tf_op jit(solution)/shard_map/ppermute | solution.py:227
  14.0 10.4 %collective-permute-start.3 = (bf16[2,4,128,256]{3,2,1,0:T(8,128)(2,1)S(1)}, bf16[2,4,128,256]{3,2,1,0:T(8,128)(2,1)S(1)}, u32[]{:S(2)}, u32[]{:S(2)}) collective-permute-start(bf16[2,4,128,256]{3,2,1,0:T(8,128)(2,1)S(1)} %collective-permute-done.2.refs_1_), channel_id=1, source_target_pairs={{0,4},{5,1},{4,8},{9,5},{8,12},{13,9},{12,14},{15,13},{14,10},{11,... | collective-permute-start | bytes 1572872 | tf_op jit(solution)/shard_map/ppermute | solution.py:253
  17.0 16.1 %all-to-all-start = ((bf16[8,40,512]{2,1,0:T(8,128)(2,1)}), bf16[8,40,512]{2,1,0:T(8,128)(2,1)S(1)}, u32[]{:S(2)}, u32[]{:S(2)}) async-start(bf16[8,40,512]{2,1,0:T(8,128)(2,1)} %maximum_maximum_fusion), calls=%async_computation | async-start | bytes 655360 | tf_op jit(solution)/shard_map/all_to_all | solution.py:304
  24.4 10.4 %collective-permute-start.7 = (bf16[2,4,128,256]{3,2,1,0:T(8,128)(2,1)S(1)}, bf16[2,4,128,256]{3,2,1,0:T(8,128)(2,1)S(1)}, u32[]{:S(2)}, u32[]{:S(2)}) collective-permute-start(bf16[2,4,128,256]{3,2,1,0:T(8,128)(2,1)S(1)} %collective-permute-done.3.refs_3_), channel_id=1, source_target_pairs={{0,4},{5,1},{4,8},{9,5},{8,12},{13,9},{12,14},{15,13},{14,10},{11,... | collective-permute-start | bytes 1572872 | tf_op jit(solution)/shard_map/ppermute | solution.py:253
  28.7 12.2 %collective-permute-start.4 = (bf16[2,4,128,256]{3,2,1,0:T(8,128)(2,1)}, bf16[2,4,128,256]{3,2,1,0:T(8,128)(2,1)S(1)}, u32[]{:S(2)}, u32[]{:S(2)}) collective-permute-start(bf16[2,4,128,256]{3,2,1,0:T(8,128)(2,1)} %pad_maximum_fusion), channel_id=1, source_target_pairs={{0,4},{5,1},{4,8},{9,5},{8,12},{13,9},{12,14},{15,13},{14,10},{11,... | collective-permute-start | bytes 1572872 | tf_op jit(solution)/shard_map/ppermute | solution.py:253
  31.9 9.0 %collective-permute-start.5 = (bf16[2,4,128,256]{3,2,1,0:T(8,128)(2,1)S(1)}, bf16[2,4,128,256]{3,2,1,0:T(8,128)(2,1)}, u32[]{:S(2)}, u32[]{:S(2)}) collective-permute-start(bf16[2,4,128,256]{3,2,1,0:T(8,128)(2,1)S(1)} %collective-permute-done.2.refs_1_), channel_id=1, source_target_pairs={{0,1},{1,0},{2,3},{3,2},{4,5},{5,4},{6,7},{7,6},{8,9},{9,8},{10,11... | collective-permute-start | bytes 1572872 | tf_op jit(solution)/shard_map/ppermute | solution.py:227
  33.3 7.6 %collective-permute-start.9 = (bf16[256,512]{1,0:T(8,128)(2,1)S(1)}, bf16[256,512]{1,0:T(8,128)(2,1)S(1)}, u32[]{:S(2)}, u32[]{:S(2)}) collective-permute-start(bf16[256,512]{1,0:T(8,128)(2,1)S(1)} %fusion.3.refs_9_), channel_id=1, source_target_pairs={{0,16},{16,0},{1,17},{17,1},{2,18},{18,2},{3,19},{19,3},{4,20},{20... | collective-permute-start | bytes 786440 | tf_op jit(solution)/shard_map/ppermute | solution.py:227
  34.9 8.6 %collective-permute-start.12 = (bf16[256,512]{1,0:T(8,128)(2,1)S(1)}, bf16[256,512]{1,0:T(8,128)(2,1)S(1)}, u32[]{:S(2)}, u32[]{:S(2)}) collective-permute-start(bf16[256,512]{1,0:T(8,128)(2,1)S(1)} %fusion.3.refs_9_), channel_id=1, source_target_pairs={{0,1},{1,0},{2,3},{3,2},{4,5},{5,4},{6,7},{7,6},{8,9},{9,8},{10,11... | collective-permute-start | bytes 786440 | tf_op jit(solution)/shard_map/ppermute | solution.py:227
  34.9 12.4 %collective-permute-start.6 = (bf16[2,4,128,256]{3,2,1,0:T(8,128)(2,1)S(1)}, bf16[2,4,128,256]{3,2,1,0:T(8,128)(2,1)S(1)}, u32[]{:S(2)}, u32[]{:S(2)}) collective-permute-start(bf16[2,4,128,256]{3,2,1,0:T(8,128)(2,1)S(1)} %collective-permute-done.3.refs_3_), channel_id=1, source_target_pairs={{0,1},{1,0},{2,3},{3,2},{4,5},{5,4},{6,7},{7,6},{8,9},{9,8},{10,11... | collective-permute-start | bytes 1572872 | tf_op jit(solution)/shard_map/ppermute | solution.py:227
  35.4 30.4 %copy-start = (bf16[3,256,256]{2,1,0:T(8,128)(2,1)S(1)}, bf16[3,256,256]{2,1,0:T(8,128)(2,1)}, u32[]{:S(2)}) copy-start(bf16[3,256,256]{2,1,0:T(8,128)(2,1)} %res_mine_ref.1) | copy-start | bytes 1179652
  40.9 6.4 %collective-permute-start.10 = (bf16[2,2,128,256]{3,2,1,0:T(8,128)(2,1)S(1)}, bf16[2,2,128,256]{3,2,1,0:T(8,128)(2,1)S(1)}, u32[]{:S(2)}, u32[]{:S(2)}) collective-permute-start(bf16[2,2,128,256]{3,2,1,0:T(8,128)(2,1)S(1)} %constant_dynamic-slice_fusion.1), channel_id=1, source_target_pairs={{0,4},{5,1},{4,8},{9,5},{8,12},{13,9},{12,14},{15,13},{14,10},{11,... | collective-permute-start | bytes 786440 | tf_op jit(solution)/shard_map/ppermute | solution.py:253
  40.9 7.9 %collective-permute-start.8 = (bf16[2,4,128,256]{3,2,1,0:T(8,128)(2,1)S(1)}, bf16[2,4,128,256]{3,2,1,0:T(8,128)(2,1)S(1)}, u32[]{:S(2)}, u32[]{:S(2)}) collective-permute-start(bf16[2,4,128,256]{3,2,1,0:T(8,128)(2,1)S(1)} %collective-permute-done.7.refs_5_), channel_id=1, source_target_pairs={{0,1},{1,0},{2,3},{3,2},{4,5},{5,4},{6,7},{7,6},{8,9},{9,8},{10,11... | collective-permute-start | bytes 1572872 | tf_op jit(solution)/shard_map/ppermute | solution.py:227
  40.9 12.0 %collective-permute-start.15 = (bf16[2,4,128,256]{3,2,1,0:T(8,128)(2,1)S(1)}, bf16[2,4,128,256]{3,2,1,0:T(8,128)(2,1)S(1)}, u32[]{:S(2)}, u32[]{:S(2)}) collective-permute-start(bf16[2,4,128,256]{3,2,1,0:T(8,128)(2,1)S(1)} %collective-permute-done.4.refs_1_), channel_id=1, source_target_pairs={{0,4},{5,1},{4,8},{9,5},{8,12},{13,9},{12,14},{15,13},{14,10},{11,... | collective-permute-start | bytes 1572872 | tf_op jit(solution)/shard_map/ppermute | solution.py:253
  43.5 3.8 %collective-permute-start.13 = (bf16[256,512]{1,0:T(8,128)(2,1)S(1)}, bf16[256,512]{1,0:T(8,128)(2,1)S(1)}, u32[]{:S(2)}, u32[]{:S(2)}) collective-permute-start(bf16[256,512]{1,0:T(8,128)(2,1)S(1)} %collective-permute-done.9.refs_11_), channel_id=1, source_target_pairs={{0,1},{1,0},{2,3},{3,2},{4,5},{5,4},{6,7},{7,6},{8,9},{9,8},{10,11... | collective-permute-start | bytes 786440 | tf_op jit(solution)/shard_map/ppermute | solution.py:227
  47.2 1.5 %collective-permute-start.11 = (bf16[2,2,128,256]{3,2,1,0:T(8,128)(2,1)S(1)}, bf16[2,2,128,256]{3,2,1,0:T(8,128)(2,1)S(1)}, u32[]{:S(2)}, u32[]{:S(2)}) collective-permute-start(bf16[2,2,128,256]{3,2,1,0:T(8,128)(2,1)S(1)} %collective-permute-done.10.refs_7_), channel_id=1, source_target_pairs={{0,1},{1,0},{2,3},{3,2},{4,5},{5,4},{6,7},{7,6},{8,9},{9,8},{10,11... | collective-permute-start | bytes 786440 | tf_op jit(solution)/shard_map/ppermute | solution.py:227
  52.9 9.2 %collective-permute-start.17 = (bf16[2,4,128,256]{3,2,1,0:T(8,128)(2,1)S(1)}, bf16[2,4,128,256]{3,2,1,0:T(8,128)(2,1)S(1)}, u32[]{:S(2)}, u32[]{:S(2)}) collective-permute-start(bf16[2,4,128,256]{3,2,1,0:T(8,128)(2,1)S(1)} %collective-permute-done.15.refs_3_), channel_id=1, source_target_pairs={{0,4},{5,1},{4,8},{9,5},{8,12},{13,9},{12,14},{15,13},{14,10},{11,... | collective-permute-start | bytes 1572872 | tf_op jit(solution)/shard_map/ppermute | solution.py:253
  52.9 9.2 %collective-permute-start.19 = (bf16[2,256,256]{2,1,0:T(8,128)(2,1)S(1)}, bf16[2,256,256]{2,1,0:T(8,128)(2,1)S(1)}, u32[]{:S(2)}, u32[]{:S(2)}) collective-permute-start(bf16[2,256,256]{2,1,0:T(8,128)(2,1)S(1)} %get-tuple-element.28), channel_id=1, source_target_pairs={{0,16},{16,0},{1,17},{17,1},{2,18},{18,2},{3,19},{19,3},{4,20},{20... | collective-permute-start | bytes 786440 | tf_op jit(solution)/shard_map/ppermute | solution.py:227
  54.4 11.4 %collective-permute-start.21 = (bf16[2,256,256]{2,1,0:T(8,128)(2,1)S(1)}, bf16[2,256,256]{2,1,0:T(8,128)(2,1)S(1)}, u32[]{:S(2)}, u32[]{:S(2)}) collective-permute-start(bf16[2,256,256]{2,1,0:T(8,128)(2,1)S(1)} %get-tuple-element.29), channel_id=1, source_target_pairs={{0,16},{16,0},{1,17},{17,1},{2,18},{18,2},{3,19},{19,3},{4,20},{20... | collective-permute-start | bytes 786440 | tf_op jit(solution)/shard_map/ppermute | solution.py:227
  62.1 6.4 %collective-permute-start.20 = (bf16[2,2,128,256]{3,2,1,0:T(8,128)(2,1)S(1)}, bf16[2,2,128,256]{3,2,1,0:T(8,128)(2,1)S(1)}, u32[]{:S(2)}, u32[]{:S(2)}) collective-permute-start(bf16[2,2,128,256]{3,2,1,0:T(8,128)(2,1)S(1)} %constant_dynamic-slice_fusion), channel_id=1, source_target_pairs={{0,4},{5,1},{4,8},{9,5},{8,12},{13,9},{12,14},{15,13},{14,10},{11,... | collective-permute-start | bytes 786440 | tf_op jit(solution)/shard_map/ppermute | solution.py:253
  64.3 5.0 %collective-permute-start.14 = (bf16[2,4,128,256]{3,2,1,0:T(8,128)(2,1)S(1)}, bf16[2,4,128,256]{3,2,1,0:T(8,128)(2,1)S(1)}, u32[]{:S(2)}, u32[]{:S(2)}) collective-permute-start(bf16[2,4,128,256]{3,2,1,0:T(8,128)(2,1)S(1)} %collective-permute-done.4.refs_1_), channel_id=1, source_target_pairs={{0,1},{1,0},{2,3},{3,2},{4,5},{5,4},{6,7},{7,6},{8,9},{9,8},{10,11... | collective-permute-start | bytes 1572872 | tf_op jit(solution)/shard_map/ppermute | solution.py:227
  64.3 5.0 %collective-permute-start.16 = (bf16[2,4,128,256]{3,2,1,0:T(8,128)(2,1)S(1)}, bf16[2,4,128,256]{3,2,1,0:T(8,128)(2,1)S(1)}, u32[]{:S(2)}, u32[]{:S(2)}) collective-permute-start(bf16[2,4,128,256]{3,2,1,0:T(8,128)(2,1)S(1)} %collective-permute-done.15.refs_3_), channel_id=1, source_target_pairs={{0,1},{1,0},{2,3},{3,2},{4,5},{5,4},{6,7},{7,6},{8,9},{9,8},{10,11... | collective-permute-start | bytes 1572872 | tf_op jit(solution)/shard_map/ppermute | solution.py:227
  64.8 5.2 %collective-permute-start.18 = (bf16[2,4,128,256]{3,2,1,0:T(8,128)(2,1)S(1)}, bf16[2,4,128,256]{3,2,1,0:T(8,128)(2,1)S(1)}, u32[]{:S(2)}, u32[]{:S(2)}) collective-permute-start(bf16[2,4,128,256]{3,2,1,0:T(8,128)(2,1)S(1)} %collective-permute-done.17.refs_5_), channel_id=1, source_target_pairs={{0,1},{1,0},{2,3},{3,2},{4,5},{5,4},{6,7},{7,6},{8,9},{9,8},{10,11... | collective-permute-start | bytes 1572872 | tf_op jit(solution)/shard_map/ppermute | solution.py:227
  65.8 6.6 %collective-permute-start.23 = (bf16[3,256,256]{2,1,0:T(8,128)(2,1)S(1)}, bf16[3,256,256]{2,1,0:T(8,128)(2,1)S(1)}, u32[]{:S(2)}, u32[]{:S(2)}) collective-permute-start(bf16[3,256,256]{2,1,0:T(8,128)(2,1)S(1)} %copy-done), channel_id=1, source_target_pairs={{0,1},{1,0},{2,3},{3,2},{4,5},{5,4},{6,7},{7,6},{8,9},{9,8},{10,11... | collective-permute-start | bytes 1179656 | tf_op jit(solution)/shard_map/ppermute | solution.py:227
  68.5 1.5 %collective-permute-start.22 = (bf16[2,2,128,256]{3,2,1,0:T(8,128)(2,1)S(1)}, bf16[2,2,128,256]{3,2,1,0:T(8,128)(2,1)S(1)}, u32[]{:S(2)}, u32[]{:S(2)}) collective-permute-start(bf16[2,2,128,256]{3,2,1,0:T(8,128)(2,1)S(1)} %collective-permute-done.20.refs_7_), channel_id=1, source_target_pairs={{0,1},{1,0},{2,3},{3,2},{4,5},{5,4},{6,7},{7,6},{8,9},{9,8},{10,11... | collective-permute-start | bytes 786440 | tf_op jit(solution)/shard_map/ppermute | solution.py:227
  69.3 3.1 %copy-start.2 = (f32[256]{0:T(256)S(1)}, f32[256]{0:T(256)}, u32[]{:S(2)}) copy-start(f32[256]{0:T(256)} %param.12) | copy-start | bytes 3076
  72.4 3.9 %copy-start.1 = (bf16[256,256]{1,0:T(8,128)(2,1)S(1)}, bf16[256,256]{1,0:T(8,128)(2,1)}, u32[]{:S(2)}) copy-start(bf16[256,256]{1,0:T(8,128)(2,1)} %skip_ref.1) | copy-start | bytes 393220
  72.4 3.8 %copy-start.3 = (f32[256]{0:T(256)S(1)}, f32[256]{0:T(256)}, u32[]{:S(2)}) copy-start(f32[256]{0:T(256)} %param.17) | copy-start | bytes 3076
  72.4 3.8 %copy-start.4 = (f32[256]{0:T(256)S(1)}, f32[256]{0:T(256)}, u32[]{:S(2)}) copy-start(f32[256]{0:T(256)} %param.19) | copy-start | bytes 3076
  73.1 3.1 %collective-permute-start.24 = (bf16[10,256,256]{2,1,0:T(8,128)(2,1)S(1)}, bf16[10,256,256]{2,1,0:T(8,128)(2,1)S(1)}, u32[]{:S(2)}, u32[]{:S(2)}) collective-permute-start(bf16[10,256,256]{2,1,0:T(8,128)(2,1)S(1)} %shard_map.115.mine_ref), channel_id=1, source_target_pairs={{0,1},{1,0},{2,3},{3,2},{4,5},{5,4},{6,7},{7,6},{8,9},{9,8},{10,11... | collective-permute-start | bytes 3932168 | tf_op jit(solution)/shard_map/ppermute | solution.py:227
  73.3 9.1 %collective-permute-start.25 = (bf16[2,256,256]{2,1,0:T(8,128)(2,1)S(1)}, bf16[2,256,256]{2,1,0:T(8,128)(2,1)S(1)}, u32[]{:S(2)}, u32[]{:S(2)}) collective-permute-start(bf16[2,256,256]{2,1,0:T(8,128)(2,1)S(1)} %get-tuple-element.33), channel_id=1, source_target_pairs={{0,16},{16,0},{1,17},{17,1},{2,18},{18,2},{3,19},{19,3},{4,20},{20... | collective-permute-start | bytes 786440 | tf_op jit(solution)/shard_map/ppermute | solution.py:227
  74.8 12.7 %collective-permute-start.26 = (bf16[2,256,256]{2,1,0:T(8,128)(2,1)S(1)}, bf16[2,256,256]{2,1,0:T(8,128)(2,1)S(1)}, u32[]{:S(2)}, u32[]{:S(2)}) collective-permute-start(bf16[2,256,256]{2,1,0:T(8,128)(2,1)S(1)} %get-tuple-element.34), channel_id=1, source_target_pairs={{0,16},{16,0},{1,17},{17,1},{2,18},{18,2},{3,19},{19,3},{4,20},{20... | collective-permute-start | bytes 786440 | tf_op jit(solution)/shard_map/ppermute | solution.py:227
where the time goes:
time: 89.8 us; the launch traced here: 89.5 us
  waiting for transfers between devices  42.5 us (47%)
  starting transfers between devices  28.8 us (32%)
  Pallas kernels  12.9 us (14%)
  other arithmetic  1.96 us (2%)
  local copies, waits for them, and re-layouts  1.78 us (2%)
  between operations  0.94 us (1%)
    ppermute x8, waiting for transfers between devices, round(): item = lax.ppermute(item, ('streams', 'segment'), self.pairs)  24.4 us
    ppermute x19, waiting for transfers between devices, swap(): return lax.ppermute(value, axis, [(0, 1), (1, 0)])  16.9 us
    ppermute x8, starting transfers between devices, round(): item = lax.ppermute(item, ('streams', 'segment'), self.pairs)  16.5 us
    ppermute x19, starting transfers between devices, swap(): return lax.ppermute(value, axis, [(0, 1), (1, 0)])  7.48 us
    pallas_call x2, Pallas kernels, spread_taps(): pl.pallas_call(functools.partial(spread_kernel, count, steps), out_shape=...  5.13 us
    pallas_call x1, Pallas kernels, residual(): pl.pallas_call(residual_kernel, out_shape=jax.ShapeDtypeStruct((sessions...  5.08 us
    all_to_all x1, starting transfers between devices, local(): lax.all_to_all(parcel, 'streams', split_axis=0, concat_axis=0, tiled=True)  4.79 us
    pallas_call x1, Pallas kernels, weave(): pl.pallas_call(weave_kernel, out_shape=jax.ShapeDtypeStruct((sessions * s...  2 us
  transfers between devices with their start and end apart: 28, of which 15 were waited for; matrix products, arithmetic and copies ran while one was open for 3% of the time, Pallas kernels for 11%

commit v1 on v0

--- a/solution.py
+++ b/solution.py
@@ -306,8 +306,9 @@
     stored = parcel[:, portion:].reshape(count * cap, half_taps, 2 * width)
 
     near_half = apply_elu(handed.astype(F32)).astype(BF16)
-    far_half = swap(near_half, "groups")
-    sides = (near_half, swap(near_half, "segment"), far_half, swap(far_half, "segment"))
+    near_other = swap(near_half, "segment")
+    far_half = swap(after(near_half, near_other), "groups")
+    sides = (near_half, near_other, far_half, swap(far_half, "segment"))
 
     slots = stored[:, history, width:].astype(jnp.int32)[:, :1]
     one_hot = (slots == jnp.arange(sessions, dtype=jnp.int32)[None, :]).astype(BF16)

time: 89.8 us -> 90.5 us (level)
  local copies, waits for them, and re-layouts: 1.78 us -> 4.76 us
  waiting for transfers between devices: 42.5 us -> 40.1 us
    ppermute x8, waiting for transfers between devices: 24.4 us -> 16.5 us  [round(): item = lax.ppermute(item, ('streams', 'segment'), self.pairs)]
    all_to_all x1, waiting for transfers between devices: 1.19 us -> 8.95 us  [local(): lax.all_to_all(parcel, 'streams', split_axis=0, concat_axis=0, tiled=True)]
    ppermute x19, waiting for transfers between devices: 16.9 us -> 14.7 us  [swap(): return lax.ppermute(value, axis, [(0, 1), (1, 0)])]
  transfers between devices with their start and end apart: 28 -> 28, of which waited for: 15 -> 17; matrix products, arithmetic and copies ran while one was open for 3% -> 6% of each run, Pallas kernels for 11% -> 11%
where the time goes in v1:
time: 90.5 us; the launch traced here: 90.1 us
  waiting for transfers between devices  40.1 us (44%)
  starting transfers between devices  28.7 us (32%)
  Pallas kernels  12.9 us (14%)
  local copies, waits for them, and re-layouts  4.76 us (5%)
  other arithmetic  1.96 us (2%)
  between operations  0.92 us (1%)
    ppermute x8, waiting for transfers between devices, round(): item = lax.ppermute(item, ('streams', 'segment'), self.pairs)  16.5 us
    ppermute x8, starting transfers between devices, round(): item = lax.ppermute(item, ('streams', 'segment'), self.pairs)  16.1 us
    ppermute x19, waiting for transfers between devices, swap(): return lax.ppermute(value, axis, [(0, 1), (1, 0)])  14.7 us
    all_to_all x1, waiting for transfers between devices, local(): lax.all_to_all(parcel, 'streams', split_axis=0, concat_axis=0, tiled=True)  8.95 us
    ppermute x19, starting transfers between devices, swap(): return lax.ppermute(value, axis, [(0, 1), (1, 0)])  7.9 us
    pallas_call x2, Pallas kernels, spread_taps(): pl.pallas_call(functools.partial(spread_kernel, count, steps), out_shape=...  5.16 us
    pallas_call x1, Pallas kernels, residual(): pl.pallas_call(residual_kernel, out_shape=jax.ShapeDtypeStruct((sessions...  5.07 us
    all_to_all x1, starting transfers between devices, local(): lax.all_to_all(parcel, 'streams', split_axis=0, concat_axis=0, tiled=True)  4.79 us
  transfers between devices with their start and end apart: 28, of which 17 were waited for; matrix products, arithmetic and copies ran while one was open for 6% of the time, Pallas kernels for 11%

profile of v1, /device:TPU:0, one launch (start us, length us, event | category | flops | bytes accessed | tf_op | source)
XLA Modules:
  0.0 90.1 jit_solution(845592715016689021)
XLA Ops:
  0.6 1.5 %constant_dynamic-slice_fusion.2 = (bf16[128,4,256]{2,1,0:T(4,128)(2,1)S(1)}, bf16[128,4,256]{2,1,0:T(4,128)(2,1)S(1)}) fusion(bf16[128,16,256]{2,1,0:T(8,128)(2,1)} %param.11, s32[]{:T(128)S(6)} %select_n.15, s32[]{:T(128)S(6)} %select_n.14), kind=kLoop, calls=%fused_computation.24 | loop fusion | bytes 1048584 | tf_op jit(solution)/shard_map/dynamic_slice | solution.py:282
  2.2 0.5 collective-permute-start
  2.7 1.2 %collective-permute-done = bf16[4,128,256]{2,1,0:T(8,128)(2,1)S(1)} collective-permute-done((bf16[4,128,256]{2,1,0:T(8,128)(2,1)S(1)}, bf16[4,128,256]{2,1,0:T(8,128)(2,1)S(1)}, u32[]{:S(2)}, u32[]{:S(2)}) %collective-permute-start) | collective-permute-done | bytes 262176 | tf_op jit(solution)/shard_map/ppermute | solution.py:227
  3.9 3.0 %collective-permute-start.2 = (bf16[2,4,128,256]{3,2,1,0:T(8,128)(2,1)S(1)}, bf16[2,4,128,256]{3,2,1,0:T(8,128)(2,1)S(1)}, u32[]{:S(2)}, u32[]{:S(2)}) collective-permute-start(bf16[2,4,128,256]{3,2,1,0:T(8,128)(2,1)S(1)} %pad_maximum_fusion.1), channel_id=1, source_target_pairs={{0,4},{5,1},{4,8},{9,5},{8,12},{13,9},{12,14},{15,13},{14,10},{11,... | collective-permute-start | bytes 1572872 | tf_op jit(solution)/shard_map/ppermute | solution.py:253
  7.2 0.8 maximum_maximum_fusion
  8.0 0.6 collective-permute-done.1
  8.6 4.8 %all-to-all-start = ((bf16[8,40,512]{2,1,0:T(8,128)(2,1)}), bf16[8,40,512]{2,1,0:T(8,128)(2,1)S(1)}, u32[]{:S(2)}, u32[]{:S(2)}) async-start(bf16[8,40,512]{2,1,0:T(8,128)(2,1)} %maximum_maximum_fusion), calls=%async_computation | async-start | bytes 655360 | tf_op jit(solution)/shard_map/all_to_all | solution.py:304
  13.4 0.6 collective-permute-done.2.refs_1_
  14.0 2.1 %collective-permute-start.3 = (bf16[2,4,128,256]{3,2,1,0:T(8,128)(2,1)S(1)}, bf16[2,4,128,256]{3,2,1,0:T(8,128)(2,1)S(1)}, u32[]{:S(2)}, u32[]{:S(2)}) collective-permute-start(bf16[2,4,128,256]{3,2,1,0:T(8,128)(2,1)S(1)} %collective-permute-done.2.refs_1_), channel_id=1, source_target_pairs={{0,4},{5,1},{4,8},{9,5},{8,12},{13,9},{12,14},{15,13},{14,10},{11,... | collective-permute-start | bytes 1572872 | tf_op jit(solution)/shard_map/ppermute | solution.py:253
  16.1 8.9 %all-to-all-done = bf16[8,40,512]{2,1,0:T(8,128)(2,1)S(1)} async-done(((bf16[8,40,512]{2,1,0:T(8,128)(2,1)}), bf16[8,40,512]{2,1,0:T(8,128)(2,1)S(1)}, u32[]{:S(2)}, u32[]{:S(2)}) %all-to-all-start) | async-done | bytes 327712 | tf_op jit(solution)/shard_map/all_to_all | solution.py:304
  25.1 0.7 copy-done.5
  25.8 2.1 %collective-permute-start.7 = (bf16[2,4,128,256]{3,2,1,0:T(8,128)(2,1)S(1)}, bf16[2,4,128,256]{3,2,1,0:T(8,128)(2,1)S(1)}, u32[]{:S(2)}, u32[]{:S(2)}) collective-permute-start(bf16[2,4,128,256]{3,2,1,0:T(8,128)(2,1)S(1)} %collective-permute-done.3.refs_3_), channel_id=1, source_target_pairs={{0,4},{5,1},{4,8},{9,5},{8,12},{13,9},{12,14},{15,13},{14,10},{11,... | collective-permute-start | bytes 1572872 | tf_op jit(solution)/shard_map/ppermute | solution.py:253
  28.2 0.8 pad_maximum_fusion
  29.0 2.5 %collective-permute-start.4 = (bf16[2,4,128,256]{3,2,1,0:T(8,128)(2,1)}, bf16[2,4,128,256]{3,2,1,0:T(8,128)(2,1)S(1)}, u32[]{:S(2)}, u32[]{:S(2)}) collective-permute-start(bf16[2,4,128,256]{3,2,1,0:T(8,128)(2,1)} %pad_maximum_fusion), channel_id=1, source_target_pairs={{0,4},{5,1},{4,8},{9,5},{8,12},{13,9},{12,14},{15,13},{14,10},{11,... | collective-permute-start | bytes 1572872 | tf_op jit(solution)/shard_map/ppermute | solution.py:253
  31.5 1.5 %collective-permute-start.10 = (bf16[256,512]{1,0:T(8,128)(2,1)S(1)}, bf16[256,512]{1,0:T(8,128)(2,1)S(1)}, u32[]{:S(2)}, u32[]{:S(2)}) collective-permute-start(bf16[256,512]{1,0:T(8,128)(2,1)S(1)} %fusion.3.refs_9_), channel_id=1, source_target_pairs={{0,16},{16,0},{1,17},{17,1},{2,18},{18,2},{3,19},{19,3},{4,20},{20... | collective-permute-start | bytes 786440 | tf_op jit(solution)/shard_map/ppermute | solution.py:227
  33.0 0.5 collective-permute-start.6
  33.6 2.0 %collective-permute-done.7.refs_5_ = bf16[2,4,128,256]{3,2,1,0:T(8,128)(2,1)S(1)} collective-permute-done((bf16[2,4,128,256]{3,2,1,0:T(8,128)(2,1)S(1)}, bf16[2,4,128,256]{3,2,1,0:T(8,128)(2,1)S(1)}, u32[]{:S(2)}, u32[]{:S(2)}) %collective-permute-start.7) | collective-permute-done | bytes 524320 | tf_op jit(solution)/shard_map/ppermute | solution.py:253
  35.6 2.9 %collective-permute-done.10.refs_11_ = bf16[256,512]{1,0:T(8,128)(2,1)S(1)} collective-permute-done((bf16[256,512]{1,0:T(8,128)(2,1)S(1)}, bf16[256,512]{1,0:T(8,128)(2,1)S(1)}, u32[]{:S(2)}, u32[]{:S(2)}) %collective-permute-start.10) | collective-permute-done | bytes 262176 | tf_op jit(solution)/shard_map/ppermute | solution.py:227
  38.5 2.0 %collective-permute-start.11 = (bf16[2,2,128,256]{3,2,1,0:T(8,128)(2,1)S(1)}, bf16[2,2,128,256]{3,2,1,0:T(8,128)(2,1)S(1)}, u32[]{:S(2)}, u32[]{:S(2)}) collective-permute-start(bf16[2,2,128,256]{3,2,1,0:T(8,128)(2,1)S(1)} %constant_dynamic-slice_fusion.1), channel_id=1, source_target_pairs={{0,4},{5,1},{4,8},{9,5},{8,12},{13,9},{12,14},{15,13},{14,10},{11,... | collective-permute-start | bytes 786440 | tf_op jit(solution)/shard_map/ppermute | solution.py:253
  40.6 0.6 collective-permute-done.4.refs_1_
  41.2 1.7 %collective-permute-start.15 = (bf16[2,4,128,256]{3,2,1,0:T(8,128)(2,1)S(1)}, bf16[2,4,128,256]{3,2,1,0:T(8,128)(2,1)S(1)}, u32[]{:S(2)}, u32[]{:S(2)}) collective-permute-start(bf16[2,4,128,256]{3,2,1,0:T(8,128)(2,1)S(1)} %collective-permute-done.4.refs_1_), channel_id=1, source_target_pairs={{0,4},{5,1},{4,8},{9,5},{8,12},{13,9},{12,14},{15,13},{14,10},{11,... | collective-permute-start | bytes 1572872 | tf_op jit(solution)/shard_map/ppermute | solution.py:253
  42.9 2.0 %collective-permute-done.11.refs_7_ = bf16[2,2,128,256]{3,2,1,0:T(8,128)(2,1)S(1)} collective-permute-done((bf16[2,2,128,256]{3,2,1,0:T(8,128)(2,1)S(1)}, bf16[2,2,128,256]{3,2,1,0:T(8,128)(2,1)S(1)}, u32[]{:S(2)}, u32[]{:S(2)}) %collective-permute-start.11) | collective-permute-done | bytes 262176 | tf_op jit(solution)/shard_map/ppermute | solution.py:253
  45.0 1.5 %collective-permute-done.12.refs_8_ = bf16[2,2,128,256]{3,2,1,0:T(8,128)(2,1)S(1)} collective-permute-done((bf16[2,2,128,256]{3,2,1,0:T(8,128)(2,1)S(1)}, bf16[2,2,128,256]{3,2,1,0:T(8,128)(2,1)S(1)}, u32[]{:S(2)}, u32[]{:S(2)}) %collective-permute-start.12) | collective-permute-done | bytes 262176 | tf_op jit(solution)/shard_map/ppermute | solution.py:227
  46.4 2.8 %shard_map.113 = (f32[4,256,256]{2,1,0:T(8,128)S(1)}, bf16[2,256,256]{2,1,0:T(8,128)(2,1)S(1)}, bf16[2,256,256]{2,1,0:T(8,128)(2,1)S(1)}) custom-call(bf16[4,128,256]{2,1,0:T(8,128)(2,1)S(1)} %bitcast.37, bf16[2,4,128,256]{3,2,1,0:T(8,128)(2,1)S(1)} %collective-permute-done.2.refs_1_, bf16[2,4,128,256]{3,2,1,0:T(8,128)(2,1)} %collective-permute-done.5.refs_2_, ...), custom_call_target="tpu_custom_call" | custom-call | flops 1073741824 | bytes 4718592 | tf_op jit(solution)/shard_map/pallas_call | solution.py:80
  49.3 2.2 %collective-permute-done.15.refs_3_ = bf16[2,4,128,256]{3,2,1,0:T(8,128)(2,1)S(1)} collective-permute-done((bf16[2,4,128,256]{3,2,1,0:T(8,128)(2,1)S(1)}, bf16[2,4,128,256]{3,2,1,0:T(8,128)(2,1)S(1)}, u32[]{:S(2)}, u32[]{:S(2)}) %collective-permute-start.15) | collective-permute-done | bytes 524320 | tf_op jit(solution)/shard_map/ppermute | solution.py:253
  51.5 1.0 %collective-permute-start.17 = (bf16[2,4,128,256]{3,2,1,0:T(8,128)(2,1)S(1)}, bf16[2,4,128,256]{3,2,1,0:T(8,128)(2,1)S(1)}, u32[]{:S(2)}, u32[]{:S(2)}) collective-permute-start(bf16[2,4,128,256]{3,2,1,0:T(8,128)(2,1)S(1)} %collective-permute-done.15.refs_3_), channel_id=1, source_target_pairs={{0,4},{5,1},{4,8},{9,5},{8,12},{13,9},{12,14},{15,13},{14,10},{11,... | collective-permute-start | bytes 1572872 | tf_op jit(solution)/shard_map/ppermute | solution.py:253
  52.5 1.5 %collective-permute-start.19 = (bf16[2,256,256]{2,1,0:T(8,128)(2,1)S(1)}, bf16[2,256,256]{2,1,0:T(8,128)(2,1)S(1)}, u32[]{:S(2)}, u32[]{:S(2)}) collective-permute-start(bf16[2,256,256]{2,1,0:T(8,128)(2,1)S(1)} %get-tuple-element.30), channel_id=1, source_target_pairs={{0,16},{16,0},{1,17},{17,1},{2,18},{18,2},{3,19},{19,3},{4,20},{20... | collective-permute-start | bytes 786440 | tf_op jit(solution)/shard_map/ppermute | solution.py:227
  54.1 0.5 collective-permute-start.21
  54.6 6.1 %collective-permute-done.17.refs_5_ = bf16[2,4,128,256]{3,2,1,0:T(8,128)(2,1)S(1)} collective-permute-done((bf16[2,4,128,256]{3,2,1,0:T(8,128)(2,1)S(1)}, bf16[2,4,128,256]{3,2,1,0:T(8,128)(2,1)S(1)}, u32[]{:S(2)}, u32[]{:S(2)}) %collective-permute-start.17) | collective-permute-done | bytes 524320 | tf_op jit(solution)/shard_map/ppermute | solution.py:253
  60.7 1.1 %collective-permute-done.19.first_ref = bf16[2,256,256]{2,1,0:T(8,128)(2,1)S(1)} collective-permute-done((bf16[2,256,256]{2,1,0:T(8,128)(2,1)S(1)}, bf16[2,256,256]{2,1,0:T(8,128)(2,1)S(1)}, u32[]{:S(2)}, u32[]{:S(2)}) %collective-permute-start.19) | collective-permute-done | bytes 262176 | tf_op jit(solution)/shard_map/ppermute | solution.py:227
  61.8 1.6 %collective-permute-start.20 = (bf16[2,2,128,256]{3,2,1,0:T(8,128)(2,1)S(1)}, bf16[2,2,128,256]{3,2,1,0:T(8,128)(2,1)S(1)}, u32[]{:S(2)}, u32[]{:S(2)}) collective-permute-start(bf16[2,2,128,256]{3,2,1,0:T(8,128)(2,1)S(1)} %constant_dynamic-slice_fusion), channel_id=1, source_target_pairs={{0,4},{5,1},{4,8},{9,5},{8,12},{13,9},{12,14},{15,13},{14,10},{11,... | collective-permute-start | bytes 786440 | tf_op jit(solution)/shard_map/ppermute | solution.py:253
  63.3 0.5 collective-permute-start.16
  63.8 0.8 slice.28
  64.6 0.7 collective-permute-done.21.second_ref
  65.3 2.8 %collective-permute-done.20.refs_7_ = bf16[2,2,128,256]{3,2,1,0:T(8,128)(2,1)S(1)} collective-permute-done((bf16[2,2,128,256]{3,2,1,0:T(8,128)(2,1)S(1)}, bf16[2,2,128,256]{3,2,1,0:T(8,128)(2,1)S(1)}, u32[]{:S(2)}, u32[]{:S(2)}) %collective-permute-start.20) | collective-permute-done | bytes 262176 | tf_op jit(solution)/shard_map/ppermute | solution.py:253
  68.3 0.8 slice.26
  69.0 0.8 slice.27
  69.8 0.6 fusion.prev_ref
  70.5 2.3 %shard_map.114 = (bf16[4,256,256]{2,1,0:T(8,128)(2,1)S(1)}, bf16[2,256,256]{2,1,0:T(8,128)(2,1)S(1)}, bf16[2,256,256]{2,1,0:T(8,128)(2,1)S(1)}) custom-call(bf16[4,128,256]{2,1,0:T(8,128)(2,1)S(1)} %bitcast.34, bf16[2,4,128,256]{3,2,1,0:T(8,128)(2,1)S(1)} %collective-permute-done.4.refs_1_, bf16[2,4,128,256]{3,2,1,0:T(8,128)(2,1)S(1)} %collective-permute-done.14.refs_2_, ...), custom_call_target="tpu_custom_call" | custom-call | flops 1073741824 | bytes 4718592 | tf_op jit(solution)/shard_map/pallas_call | solution.py:80
  72.9 0.7 shard_map.115.mine_ref
  73.6 0.6 collective-permute-start.24
  74.2 1.5 %collective-permute-start.25 = (bf16[2,256,256]{2,1,0:T(8,128)(2,1)S(1)}, bf16[2,256,256]{2,1,0:T(8,128)(2,1)S(1)}, u32[]{:S(2)}, u32[]{:S(2)}) collective-permute-start(bf16[2,256,256]{2,1,0:T(8,128)(2,1)S(1)} %get-tuple-element.35), channel_id=1, source_target_pairs={{0,16},{16,0},{1,17},{17,1},{2,18},{18,2},{3,19},{19,3},{4,20},{20... | collective-permute-start | bytes 786440 | tf_op jit(solution)/shard_map/ppermute | solution.py:227
  75.7 0.5 collective-permute-start.26
  76.2 0.6 collective-permute-done.24.theirs_ref
  76.8 5.1 %shard_map.116 = bf16[2048,256]{1,0:T(8,128)(2,1)} custom-call(s32[1]{0:T(128)} %bitcast.group_ref, f32[4,256,256]{2,1,0:T(8,128)S(1)} %get-tuple-element.37.own_ref, bf16[2,256,256]{2,1,0:T(8,128)(2,1)S(1)} %collective-permute-done.19.first_ref, bf16[2,256,256]{2,1,0:T(8,128)(2,1)S(1)} %collective-permute-done.21.second_ref, ...), custom_call_target="tpu_custom_call" | custom-call | tf_op jit(solution)/shard_map/pallas_call | solution.py:183
  81.9 1.4 %collective-permute-done.25.first_ref = bf16[2,256,256]{2,1,0:T(8,128)(2,1)S(1)} collective-permute-done((bf16[2,256,256]{2,1,0:T(8,128)(2,1)S(1)}, bf16[2,256,256]{2,1,0:T(8,128)(2,1)S(1)}, u32[]{:S(2)}, u32[]{:S(2)}) %collective-permute-start.25) | collective-permute-done | bytes 262176 | tf_op jit(solution)/shard_map/ppermute | solution.py:227
  83.3 4.7 %collective-permute-done.26.second_ref = bf16[2,256,256]{2,1,0:T(8,128)(2,1)S(1)} collective-permute-done((bf16[2,256,256]{2,1,0:T(8,128)(2,1)S(1)}, bf16[2,256,256]{2,1,0:T(8,128)(2,1)S(1)}, u32[]{:S(2)}, u32[]{:S(2)}) %collective-permute-start.26) | collective-permute-done | bytes 262176 | tf_op jit(solution)/shard_map/ppermute | solution.py:227
  88.1 2.0 %shard_map.117 = bf16[2048,256]{1,0:T(8,128)(2,1)} custom-call(s32[1]{0:T(128)} %bitcast.group_ref, bf16[4,256,256]{2,1,0:T(8,128)(2,1)S(1)} %get-tuple-element.39.own_ref, bf16[2,256,256]{2,1,0:T(8,128)(2,1)S(1)} %collective-permute-done.25.first_ref, bf16[2,256,256]{2,1,0:T(8,128)(2,1)S(1)} %collective-permute-done.26.second_ref), custom_call_target="tpu_custom_call" | custom-call | tf_op jit(solution)/shard_map/pallas_call | solution.py:215
  (55 shorter events, 0.9 us)
Async XLA Ops:
  2.1 4.9 %copy-start.9 = (s32[8]{0:T(128)S(1)}, s32[8]{0:T(128)}, u32[]{:S(2)}) copy-start(s32[8]{0:T(128)} %param.15) | copy-start | bytes 100
  2.1 5.0 %copy-start.6 = (bf16[256,512]{1,0:T(8,128)(2,1)S(1)}, bf16[256,512]{1,0:T(8,128)(2,1)}, u32[]{:S(2)}) copy-start(bf16[256,512]{1,0:T(8,128)(2,1)} %param.10) | copy-start | bytes 786436
  2.1 5.0 %copy-start.7 = (bf16[8,8,256]{2,1,0:T(8,128)(2,1)S(1)}, bf16[8,8,256]{2,1,0:T(8,128)(2,1)}, u32[]{:S(2)}) copy-start(bf16[8,8,256]{2,1,0:T(8,128)(2,1)} %param.13) | copy-start | bytes 98308
  2.2 5.0 %copy-start.8 = (bf16[8,2,256]{2,1,0:T(2,128)(2,1)S(1)}, bf16[8,2,256]{2,1,0:T(2,128)(2,1)}, u32[]{:S(2)}) copy-start(bf16[8,2,256]{2,1,0:T(2,128)(2,1)} %param.14) | copy-start | bytes 24580
  2.2 1.7 %collective-permute-start = (bf16[4,128,256]{2,1,0:T(8,128)(2,1)S(1)}, bf16[4,128,256]{2,1,0:T(8,128)(2,1)S(1)}, u32[]{:S(2)}, u32[]{:S(2)}) collective-permute-start(bf16[4,128,256]{2,1,0:T(8,128)(2,1)S(1)} %bitcast.35), channel_id=1, source_target_pairs={{0,1},{1,0},{2,3},{3,2},{4,5},{5,4},{6,7},{7,6},{8,9},{9,8},{10,11... | collective-permute-start | bytes 786440 | tf_op jit(solution)/shard_map/ppermute | solution.py:227
  3.9 10.1 %collective-permute-start.2 = (bf16[2,4,128,256]{3,2,1,0:T(8,128)(2,1)S(1)}, bf16[2,4,128,256]{3,2,1,0:T(8,128)(2,1)S(1)}, u32[]{:S(2)}, u32[]{:S(2)}) collective-permute-start(bf16[2,4,128,256]{3,2,1,0:T(8,128)(2,1)S(1)} %pad_maximum_fusion.1), channel_id=1, source_target_pairs={{0,4},{5,1},{4,8},{9,5},{8,12},{13,9},{12,14},{15,13},{14,10},{11,... | collective-permute-start | bytes 1572872 | tf_op jit(solution)/shard_map/ppermute | solution.py:253
  7.0 1.6 %collective-permute-start.1 = (bf16[4,128,256]{2,1,0:T(8,128)(2,1)S(1)}, bf16[4,128,256]{2,1,0:T(8,128)(2,1)S(1)}, u32[]{:S(2)}, u32[]{:S(2)}) collective-permute-start(bf16[4,128,256]{2,1,0:T(8,128)(2,1)S(1)} %bitcast.32), channel_id=1, source_target_pairs={{0,1},{1,0},{2,3},{3,2},{4,5},{5,4},{6,7},{7,6},{8,9},{9,8},{10,11... | collective-permute-start | bytes 786440 | tf_op jit(solution)/shard_map/ppermute | solution.py:227
  8.6 16.5 %all-to-all-start = ((bf16[8,40,512]{2,1,0:T(8,128)(2,1)}), bf16[8,40,512]{2,1,0:T(8,128)(2,1)S(1)}, u32[]{:S(2)}, u32[]{:S(2)}) async-start(bf16[8,40,512]{2,1,0:T(8,128)(2,1)} %maximum_maximum_fusion), calls=%async_computation | async-start | bytes 655360 | tf_op jit(solution)/shard_map/all_to_all | solution.py:304
  14.0 11.8 %collective-permute-start.3 = (bf16[2,4,128,256]{3,2,1,0:T(8,128)(2,1)S(1)}, bf16[2,4,128,256]{3,2,1,0:T(8,128)(2,1)S(1)}, u32[]{:S(2)}, u32[]{:S(2)}) collective-permute-start(bf16[2,4,128,256]{3,2,1,0:T(8,128)(2,1)S(1)} %collective-permute-done.2.refs_1_), channel_id=1, source_target_pairs={{0,4},{5,1},{4,8},{9,5},{8,12},{13,9},{12,14},{15,13},{14,10},{11,... | collective-permute-start | bytes 1572872 | tf_op jit(solution)/shard_map/ppermute | solution.py:253
  25.1 0.7 copy-start.5
  25.8 9.7 %collective-permute-start.7 = (bf16[2,4,128,256]{3,2,1,0:T(8,128)(2,1)S(1)}, bf16[2,4,128,256]{3,2,1,0:T(8,128)(2,1)S(1)}, u32[]{:S(2)}, u32[]{:S(2)}) collective-permute-start(bf16[2,4,128,256]{3,2,1,0:T(8,128)(2,1)S(1)} %collective-permute-done.3.refs_3_), channel_id=1, source_target_pairs={{0,4},{5,1},{4,8},{9,5},{8,12},{13,9},{12,14},{15,13},{14,10},{11,... | collective-permute-start | bytes 1572872 | tf_op jit(solution)/shard_map/ppermute | solution.py:253
  28.1 3.4 %collective-permute-start.9 = (bf16[256,512]{1,0:T(8,128)(2,1)S(1)}, bf16[256,512]{1,0:T(8,128)(2,1)S(1)}, u32[]{:S(2)}, u32[]{:S(2)}) collective-permute-start(bf16[256,512]{1,0:T(8,128)(2,1)S(1)} %fusion.3.refs_9_), channel_id=1, source_target_pairs={{0,1},{1,0},{2,3},{3,2},{4,5},{5,4},{6,7},{7,6},{8,9},{9,8},{10,11... | collective-permute-start | bytes 786440 | tf_op jit(solution)/shard_map/ppermute | solution.py:227
  29.0 12.1 %collective-permute-start.4 = (bf16[2,4,128,256]{3,2,1,0:T(8,128)(2,1)}, bf16[2,4,128,256]{3,2,1,0:T(8,128)(2,1)S(1)}, u32[]{:S(2)}, u32[]{:S(2)}) collective-permute-start(bf16[2,4,128,256]{3,2,1,0:T(8,128)(2,1)} %pad_maximum_fusion), channel_id=1, source_target_pairs={{0,4},{5,1},{4,8},{9,5},{8,12},{13,9},{12,14},{15,13},{14,10},{11,... | collective-permute-start | bytes 1572872 | tf_op jit(solution)/shard_map/ppermute | solution.py:253
  31.5 7.0 %collective-permute-start.10 = (bf16[256,512]{1,0:T(8,128)(2,1)S(1)}, bf16[256,512]{1,0:T(8,128)(2,1)S(1)}, u32[]{:S(2)}, u32[]{:S(2)}) collective-permute-start(bf16[256,512]{1,0:T(8,128)(2,1)S(1)} %fusion.3.refs_9_), channel_id=1, source_target_pairs={{0,16},{16,0},{1,17},{17,1},{2,18},{18,2},{3,19},{19,3},{4,20},{20... | collective-permute-start | bytes 786440 | tf_op jit(solution)/shard_map/ppermute | solution.py:227
  33.0 9.8 %collective-permute-start.5 = (bf16[2,4,128,256]{3,2,1,0:T(8,128)(2,1)S(1)}, bf16[2,4,128,256]{3,2,1,0:T(8,128)(2,1)}, u32[]{:S(2)}, u32[]{:S(2)}) collective-permute-start(bf16[2,4,128,256]{3,2,1,0:T(8,128)(2,1)S(1)} %collective-permute-done.2.refs_1_), channel_id=1, source_target_pairs={{0,1},{1,0},{2,3},{3,2},{4,5},{5,4},{6,7},{7,6},{8,9},{9,8},{10,11... | collective-permute-start | bytes 1572872 | tf_op jit(solution)/shard_map/ppermute | solution.py:227
  33.0 11.9 %collective-permute-start.6 = (bf16[2,4,128,256]{3,2,1,0:T(8,128)(2,1)S(1)}, bf16[2,4,128,256]{3,2,1,0:T(8,128)(2,1)S(1)}, u32[]{:S(2)}, u32[]{:S(2)}) collective-permute-start(bf16[2,4,128,256]{3,2,1,0:T(8,128)(2,1)S(1)} %collective-permute-done.3.refs_3_), channel_id=1, source_target_pairs={{0,1},{1,0},{2,3},{3,2},{4,5},{5,4},{6,7},{7,6},{8,9},{9,8},{10,11... | collective-permute-start | bytes 1572872 | tf_op jit(solution)/shard_map/ppermute | solution.py:227
  35.6 29.7 %copy-start = (bf16[3,256,256]{2,1,0:T(8,128)(2,1)S(1)}, bf16[3,256,256]{2,1,0:T(8,128)(2,1)}, u32[]{:S(2)}) copy-start(bf16[3,256,256]{2,1,0:T(8,128)(2,1)} %res_mine_ref.1) | copy-start | bytes 1179652
  38.5 6.4 %collective-permute-start.11 = (bf16[2,2,128,256]{3,2,1,0:T(8,128)(2,1)S(1)}, bf16[2,2,128,256]{3,2,1,0:T(8,128)(2,1)S(1)}, u32[]{:S(2)}, u32[]{:S(2)}) collective-permute-start(bf16[2,2,128,256]{3,2,1,0:T(8,128)(2,1)S(1)} %constant_dynamic-slice_fusion.1), channel_id=1, source_target_pairs={{0,4},{5,1},{4,8},{9,5},{8,12},{13,9},{12,14},{15,13},{14,10},{11,... | collective-permute-start | bytes 786440 | tf_op jit(solution)/shard_map/ppermute | solution.py:253
  40.5 5.9 %collective-permute-start.8 = (bf16[2,4,128,256]{3,2,1,0:T(8,128)(2,1)S(1)}, bf16[2,4,128,256]{3,2,1,0:T(8,128)(2,1)S(1)}, u32[]{:S(2)}, u32[]{:S(2)}) collective-permute-start(bf16[2,4,128,256]{3,2,1,0:T(8,128)(2,1)S(1)} %collective-permute-done.7.refs_5_), channel_id=1, source_target_pairs={{0,1},{1,0},{2,3},{3,2},{4,5},{5,4},{6,7},{7,6},{8,9},{9,8},{10,11... | collective-permute-start | bytes 1572872 | tf_op jit(solution)/shard_map/ppermute | solution.py:227
  41.2 10.4 %collective-permute-start.15 = (bf16[2,4,128,256]{3,2,1,0:T(8,128)(2,1)S(1)}, bf16[2,4,128,256]{3,2,1,0:T(8,128)(2,1)S(1)}, u32[]{:S(2)}, u32[]{:S(2)}) collective-permute-start(bf16[2,4,128,256]{3,2,1,0:T(8,128)(2,1)S(1)} %collective-permute-done.4.refs_1_), channel_id=1, source_target_pairs={{0,4},{5,1},{4,8},{9,5},{8,12},{13,9},{12,14},{15,13},{14,10},{11,... | collective-permute-start | bytes 1572872 | tf_op jit(solution)/shard_map/ppermute | solution.py:253
  42.9 2.1 %collective-permute-start.13 = (bf16[256,512]{1,0:T(8,128)(2,1)S(1)}, bf16[256,512]{1,0:T(8,128)(2,1)S(1)}, u32[]{:S(2)}, u32[]{:S(2)}) collective-permute-start(bf16[256,512]{1,0:T(8,128)(2,1)S(1)} %collective-permute-done.10.refs_11_), channel_id=1, source_target_pairs={{0,1},{1,0},{2,3},{3,2},{4,5},{5,4},{6,7},{7,6},{8,9},{9,8},{10,11... | collective-permute-start | bytes 786440 | tf_op jit(solution)/shard_map/ppermute | solution.py:227
  44.9 1.5 %collective-permute-start.12 = (bf16[2,2,128,256]{3,2,1,0:T(8,128)(2,1)S(1)}, bf16[2,2,128,256]{3,2,1,0:T(8,128)(2,1)S(1)}, u32[]{:S(2)}, u32[]{:S(2)}) collective-permute-start(bf16[2,2,128,256]{3,2,1,0:T(8,128)(2,1)S(1)} %collective-permute-done.11.refs_7_), channel_id=1, source_target_pairs={{0,1},{1,0},{2,3},{3,2},{4,5},{5,4},{6,7},{7,6},{8,9},{9,8},{10,11... | collective-permute-start | bytes 786440 | tf_op jit(solution)/shard_map/ppermute | solution.py:227
  51.5 9.2 %collective-permute-start.17 = (bf16[2,4,128,256]{3,2,1,0:T(8,128)(2,1)S(1)}, bf16[2,4,128,256]{3,2,1,0:T(8,128)(2,1)S(1)}, u32[]{:S(2)}, u32[]{:S(2)}) collective-permute-start(bf16[2,4,128,256]{3,2,1,0:T(8,128)(2,1)S(1)} %collective-permute-done.15.refs_3_), channel_id=1, source_target_pairs={{0,4},{5,1},{4,8},{9,5},{8,12},{13,9},{12,14},{15,13},{14,10},{11,... | collective-permute-start | bytes 1572872 | tf_op jit(solution)/shard_map/ppermute | solution.py:253
  52.5 9.2 %collective-permute-start.19 = (bf16[2,256,256]{2,1,0:T(8,128)(2,1)S(1)}, bf16[2,256,256]{2,1,0:T(8,128)(2,1)S(1)}, u32[]{:S(2)}, u32[]{:S(2)}) collective-permute-start(bf16[2,256,256]{2,1,0:T(8,128)(2,1)S(1)} %get-tuple-element.30), channel_id=1, source_target_pairs={{0,16},{16,0},{1,17},{17,1},{2,18},{18,2},{3,19},{19,3},{4,20},{20... | collective-permute-start | bytes 786440 | tf_op jit(solution)/shard_map/ppermute | solution.py:227
  54.1 11.3 %collective-permute-start.21 = (bf16[2,256,256]{2,1,0:T(8,128)(2,1)S(1)}, bf16[2,256,256]{2,1,0:T(8,128)(2,1)S(1)}, u32[]{:S(2)}, u32[]{:S(2)}) collective-permute-start(bf16[2,256,256]{2,1,0:T(8,128)(2,1)S(1)} %get-tuple-element.31), channel_id=1, source_target_pairs={{0,16},{16,0},{1,17},{17,1},{2,18},{18,2},{3,19},{19,3},{4,20},{20... | collective-permute-start | bytes 786440 | tf_op jit(solution)/shard_map/ppermute | solution.py:227
  61.8 6.4 %collective-permute-start.20 = (bf16[2,2,128,256]{3,2,1,0:T(8,128)(2,1)S(1)}, bf16[2,2,128,256]{3,2,1,0:T(8,128)(2,1)S(1)}, u32[]{:S(2)}, u32[]{:S(2)}) collective-permute-start(bf16[2,2,128,256]{3,2,1,0:T(8,128)(2,1)S(1)} %constant_dynamic-slice_fusion), channel_id=1, source_target_pairs={{0,4},{5,1},{4,8},{9,5},{8,12},{13,9},{12,14},{15,13},{14,10},{11,... | collective-permute-start | bytes 786440 | tf_op jit(solution)/shard_map/ppermute | solution.py:253
  63.3 7.1 %collective-permute-start.14 = (bf16[2,4,128,256]{3,2,1,0:T(8,128)(2,1)S(1)}, bf16[2,4,128,256]{3,2,1,0:T(8,128)(2,1)S(1)}, u32[]{:S(2)}, u32[]{:S(2)}) collective-permute-start(bf16[2,4,128,256]{3,2,1,0:T(8,128)(2,1)S(1)} %collective-permute-done.4.refs_1_), channel_id=1, source_target_pairs={{0,1},{1,0},{2,3},{3,2},{4,5},{5,4},{6,7},{7,6},{8,9},{9,8},{10,11... | collective-permute-start | bytes 1572872 | tf_op jit(solution)/shard_map/ppermute | solution.py:227
  63.3 7.1 %collective-permute-start.16 = (bf16[2,4,128,256]{3,2,1,0:T(8,128)(2,1)S(1)}, bf16[2,4,128,256]{3,2,1,0:T(8,128)(2,1)S(1)}, u32[]{:S(2)}, u32[]{:S(2)}) collective-permute-start(bf16[2,4,128,256]{3,2,1,0:T(8,128)(2,1)S(1)} %collective-permute-done.15.refs_3_), channel_id=1, source_target_pairs={{0,1},{1,0},{2,3},{3,2},{4,5},{5,4},{6,7},{7,6},{8,9},{9,8},{10,11... | collective-permute-start | bytes 1572872 | tf_op jit(solution)/shard_map/ppermute | solution.py:227
  63.8 6.6 %collective-permute-start.18 = (bf16[2,4,128,256]{3,2,1,0:T(8,128)(2,1)S(1)}, bf16[2,4,128,256]{3,2,1,0:T(8,128)(2,1)S(1)}, u32[]{:S(2)}, u32[]{:S(2)}) collective-permute-start(bf16[2,4,128,256]{3,2,1,0:T(8,128)(2,1)S(1)} %collective-permute-done.17.refs_5_), channel_id=1, source_target_pairs={{0,1},{1,0},{2,3},{3,2},{4,5},{5,4},{6,7},{7,6},{8,9},{9,8},{10,11... | collective-permute-start | bytes 1572872 | tf_op jit(solution)/shard_map/ppermute | solution.py:227
  65.3 7.5 %collective-permute-start.23 = (bf16[3,256,256]{2,1,0:T(8,128)(2,1)S(1)}, bf16[3,256,256]{2,1,0:T(8,128)(2,1)S(1)}, u32[]{:S(2)}, u32[]{:S(2)}) collective-permute-start(bf16[3,256,256]{2,1,0:T(8,128)(2,1)S(1)} %copy-done), channel_id=1, source_target_pairs={{0,1},{1,0},{2,3},{3,2},{4,5},{5,4},{6,7},{7,6},{8,9},{9,8},{10,11... | collective-permute-start | bytes 1179656 | tf_op jit(solution)/shard_map/ppermute | solution.py:227
  68.2 2.3 %collective-permute-start.22 = (bf16[2,2,128,256]{3,2,1,0:T(8,128)(2,1)S(1)}, bf16[2,2,128,256]{3,2,1,0:T(8,128)(2,1)S(1)}, u32[]{:S(2)}, u32[]{:S(2)}) collective-permute-start(bf16[2,2,128,256]{3,2,1,0:T(8,128)(2,1)S(1)} %collective-permute-done.20.refs_7_), channel_id=1, source_target_pairs={{0,1},{1,0},{2,3},{3,2},{4,5},{5,4},{6,7},{7,6},{8,9},{9,8},{10,11... | collective-permute-start | bytes 786440 | tf_op jit(solution)/shard_map/ppermute | solution.py:227
  70.4 2.4 %copy-start.2 = (f32[256]{0:T(256)S(1)}, f32[256]{0:T(256)}, u32[]{:S(2)}) copy-start(f32[256]{0:T(256)} %param.12) | copy-start | bytes 3076
  72.8 4.0 %copy-start.1 = (bf16[256,256]{1,0:T(8,128)(2,1)S(1)}, bf16[256,256]{1,0:T(8,128)(2,1)}, u32[]{:S(2)}) copy-start(bf16[256,256]{1,0:T(8,128)(2,1)} %skip_ref.1) | copy-start | bytes 393220
  72.9 4.0 %copy-start.3 = (f32[256]{0:T(256)S(1)}, f32[256]{0:T(256)}, u32[]{:S(2)}) copy-start(f32[256]{0:T(256)} %param.17) | copy-start | bytes 3076
  72.9 4.0 %copy-start.4 = (f32[256]{0:T(256)S(1)}, f32[256]{0:T(256)}, u32[]{:S(2)}) copy-start(f32[256]{0:T(256)} %param.19) | copy-start | bytes 3076
  73.6 3.2 %collective-permute-start.24 = (bf16[10,256,256]{2,1,0:T(8,128)(2,1)S(1)}, bf16[10,256,256]{2,1,0:T(8,128)(2,1)S(1)}, u32[]{:S(2)}, u32[]{:S(2)}) collective-permute-start(bf16[10,256,256]{2,1,0:T(8,128)(2,1)S(1)} %shard_map.115.mine_ref), channel_id=1, source_target_pairs={{0,1},{1,0},{2,3},{3,2},{4,5},{5,4},{6,7},{7,6},{8,9},{9,8},{10,11... | collective-permute-start | bytes 3932168 | tf_op jit(solution)/shard_map/ppermute | solution.py:227
  74.2 9.2 %collective-permute-start.25 = (bf16[2,256,256]{2,1,0:T(8,128)(2,1)S(1)}, bf16[2,256,256]{2,1,0:T(8,128)(2,1)S(1)}, u32[]{:S(2)}, u32[]{:S(2)}) collective-permute-start(bf16[2,256,256]{2,1,0:T(8,128)(2,1)S(1)} %get-tuple-element.35), channel_id=1, source_target_pairs={{0,16},{16,0},{1,17},{17,1},{2,18},{18,2},{3,19},{19,3},{4,20},{20... | collective-permute-start | bytes 786440 | tf_op jit(solution)/shard_map/ppermute | solution.py:227
  75.7 12.4 %collective-permute-start.26 = (bf16[2,256,256]{2,1,0:T(8,128)(2,1)S(1)}, bf16[2,256,256]{2,1,0:T(8,128)(2,1)S(1)}, u32[]{:S(2)}, u32[]{:S(2)}) collective-permute-start(bf16[2,256,256]{2,1,0:T(8,128)(2,1)S(1)} %get-tuple-element.36), channel_id=1, source_target_pairs={{0,16},{16,0},{1,17},{17,1},{2,18},{18,2},{3,19},{19,3},{4,20},{20... | collective-permute-start | bytes 786440 | tf_op jit(solution)/shard_map/ppermute | solution.py:227
